TPU v7x, 512 devices: a whole 4x4x16 slice. The times are simulated.
512 devices in a mesh: row: 16 (over y, z_hi, core), col: 32 (over z_lo, x).
Axes of the slice: x: 4, y: 4, z: 16 (z_hi: 2, z_lo: 8; z = z_hi * 8 + z_lo), core: 2. Of those that a mesh axis runs over, the one named last changes fastest.
Arguments:
- grad_out: bfloat16 [512, 16384], P('row', 'col'), may hold values from -6 to 6
- gate_pre: bfloat16 [512, 26624], P('col', 'row'), may hold values from -6 to 6
- up_pre: bfloat16 [512, 26624], P('col', 'row'), may hold values from -6 to 6
- weight_values: bfloat16 [26624, 16384], P('row', 'col'), may hold values from -0.0390625 to 0.0390625
- weight_scales: float32 [512, 26624], P('col', 'row'), may hold values from 0.25 to 4, as said below
Outputs:
- weight_grad: bfloat16 [26624, 16384], P('row', 'col')
- gate_grad: bfloat16 [512, 26624], P('col', 'row')
- up_grad: bfloat16 [512, 26624], P('col', 'row')
Inputs may be any that keep to these rules, and one draw needn't show every extreme that they name: `weight_scales`: every scale is a power of two.
All inputs are finite; a program needn't handle non-finite values.
Results may differ from a plain program's by a relative error of at most 0.006.
Values may be sent and summed in bfloat16 or wider, within the bound.
No kernel may reach another device: no remote copies, remote signals or barrier semaphores. Data moves between devices by JAX's collectives and lax.ppermute only.
A program may use at most 64 MiB of HBM per device.

v0:
```python
import jax
import jax.numpy as jnp
from jax import lax
from jax.sharding import PartitionSpec as P

BLOCK = 32


def per_device(grad_out, gate_pre, up_pre, weight_values, weight_scales):
    gate_f = gate_pre.astype(jnp.float32)
    up_f = up_pre.astype(jnp.float32)
    sig = jax.nn.sigmoid(gate_f)
    act = gate_f * sig
    hidden = (act * up_f).astype(jnp.bfloat16)
    scale_rows = jnp.repeat(weight_scales, BLOCK, axis=0)
    weight = (weight_values.astype(jnp.float32) * jnp.transpose(scale_rows)).astype(jnp.bfloat16)
    all_hidden = lax.all_gather(hidden, "col", axis=0, tiled=True)
    all_grads = lax.all_gather(grad_out, "row", axis=0, tiled=True)
    weight_sum = lax.dot_general(
        all_hidden, all_grads, (((0,), (0,)), ((), ())), preferred_element_type=jnp.float32
    )
    hidden_grad = lax.psum_scatter(
        lax.dot_general(
            all_grads, weight, (((1,), (1,)), ((), ())), preferred_element_type=jnp.float32
        ),
        "col",
        scatter_dimension=0,
        tiled=True,
    )
    weight_grad = weight_sum.astype(jnp.bfloat16)
    gate_grad = (hidden_grad * up_f * sig * (1.0 + gate_f * (1.0 - sig))).astype(jnp.bfloat16)
    up_grad = (hidden_grad * act).astype(jnp.bfloat16)
    return (weight_grad, gate_grad, up_grad)


def solution(mesh):
    placed = (P("row", "col"), P("col", "row"), P("col", "row"), P("row", "col"), P("col", "row"))
    return jax.shard_map(
        per_device,
        mesh=mesh,
        in_specs=placed,
        out_specs=(P("row", "col"), P("col", "row"), P("col", "row")),
        check_vma=False,
    )
```

profile of v0, /device:TPU:2, one launch (start us, length us, event | category | flops | bytes accessed | tf_op | source)
XLA Modules:
  0.0 544.8 jit_solution(17570113509008171970)
XLA Ops:
  7.2 0.0 reduce-scatter.4.cloned.1.call-start
  7.2 63.0 %all_gather.7 = bf16[512,512]{1,0:T(8,128)(2,1)} all-gather(bf16[32,512]{1,0:T(8,128)(2,1)} %param.5), channel_id=1, replica_groups=mesh['row'=16,'col'=32] {'row'}, dimensions={0}, use_global_device_ids=true | all-gather | bytes 557056 | tf_op jit(solution)/shard_map/all_gather | solution.py:18
  70.2 0.0 copy-start.2
  70.2 2.8 copy.18
  73.0 0.0 copy-done.2
  73.0 0.0 copy-start
  73.0 0.3 fusion
  73.3 0.7 copy-done
  74.0 1.1 convolution_bitcast_fusion
  75.1 3.1 copy.21
  78.2 0.0 copy-start.3
  78.2 0.0 copy-start.4
  78.3 0.0 copy-start.1
  78.3 0.0 reduce-scatter.4.cloned.1.call-update
  78.3 0.0 all-gather.2.cloned.1.call-start
  78.3 228.9 %reduce-scatter.4.cloned.1.call-done = f32[16,1664]{1,0:T(8,128)} async-done(((f32[512,1664]{1,0:T(8,128)}), f32[16,1664]{1,0:T(8,128)}) %reduce-scatter.4.cloned.1.call-update) | async-done | bytes 106512 | tf_op jit(solution)/shard_map/reduce_scatter | solution.py:22
  307.3 0.0 copy-done.3
  307.3 0.0 copy-done.4
  307.3 1.6 multiply_convert_fusion
  308.9 0.0 all-gather.2.cloned.1.call-update
  308.9 225.4 %all-gather.2.cloned.1.call-done = bf16[512,1664]{1,0:T(8,128)(2,1)} async-done(((bf16[16,1664]{1,0:T(8,128)(2,1)}), bf16[512,1664]{1,0:T(8,128)(2,1)}) %all-gather.2.cloned.1.call-update) | async-done | bytes 1703952 | tf_op jit(solution)/shard_map/all_gather | solution.py:17
  534.3 0.0 copy-done.1
  534.3 3.7 convolution_convert_fusion
Async XLA Ops:
  7.2 300.1 %reduce-scatter.4.cloned.1.call-start = ((), (), s32[]{:S(2)}) async-start(), calls=%async_computation.2 | async-start | bytes 3514368 | tf_op jit(solution)/shard_map/reduce_scatter | solution.py:22
  70.2 2.8 copy-start.2
  73.0 1.0 copy-start
  78.2 229.0 %copy-start.3 = (bf16[16,1664]{1,0:T(8,128)(2,1)S(1)}, bf16[16,1664]{1,0:T(8,128)(2,1)}, u32[]{:S(2)}) copy-start(bf16[16,1664]{1,0:T(8,128)(2,1)} %param.6) | copy-start | bytes 159748
  78.2 229.0 %copy-start.4 = (bf16[16,1664]{1,0:T(8,128)(2,1)S(1)}, bf16[16,1664]{1,0:T(8,128)(2,1)}, u32[]{:S(2)}) copy-start(bf16[16,1664]{1,0:T(8,128)(2,1)} %param.7) | copy-start | bytes 159748
  78.3 456.0 %copy-start.1 = (bf16[512,512]{1,0:T(8,128)(2,1)S(1)}, bf16[512,512]{1,0:T(8,128)(2,1)}, u32[]{:S(2)}) copy-start(bf16[512,512]{1,0:T(8,128)(2,1)} %all_gather.7) | copy-start | bytes 1572868
  78.3 456.0 %all-gather.2.cloned.1.call-start = ((), (), s32[]{:S(2)}) async-start(), calls=%async_computation.1 | async-start | bytes 1757184 | tf_op jit(solution)/shard_map/all_gather | solution.py:17
Sparse Core Ops, SparseCore 0:
  78.4 228.8 reduce-scatter.3
  310.1 224.1 all-gather.1
where the time goes:
time: 545 us
  waiting for transfers between devices  454 us (83%)
  blocking collectives  63 us (12%)
  between operations  14.1 us (3%)
  local copies, waits for them, and re-layouts  6.65 us (1%)
    reduce_scatter x1, waiting for transfers between devices, per_device(): lax.psum_scatter(lax.dot_general(all_grads, weight, (((1,), (1,)), ((), (...  229 us
    all_gather x1, waiting for transfers between devices, per_device(): all_hidden = lax.all_gather(hidden, 'col', axis=0, tiled=True)  225 us
    all_gather x1, blocking collectives, per_device(): all_grads = lax.all_gather(grad_out, 'row', axis=0, tiled=True)  63 us
  transfers between devices with their start and end apart: 2, of which 2 were waited for; matrix products, arithmetic and copies ran while one was open for 0% of the time, Pallas kernels for 0%

commit v1 on v0

v1 whole, which is shorter than its diff:
```python
import jax
import jax.numpy as jnp
from jax import lax
from jax.sharding import Mesh, PartitionSpec as P

BLOCK = 32


def exchange(parts, axes):
    return lax.all_to_all(parts, axes, split_axis=0, concat_axis=0)


def gather(block, axes, count):
    return exchange(jnp.broadcast_to(block[None], (count,) + block.shape), axes)


def per_device(grad_out, gate_pre, up_pre, weight_values, weight_scales):
    units = gate_pre.shape[1]
    width = grad_out.shape[1]
    gate_f = gate_pre.astype(jnp.float32)
    up_f = up_pre.astype(jnp.float32)
    sig = jax.nn.sigmoid(gate_f)
    act = gate_f * sig
    hidden = (act * up_f).astype(jnp.bfloat16)

    other = lax.ppermute(grad_out, "zh", [(0, 1), (1, 0)])
    upper = lax.axis_index("zh") == 1
    pair = jnp.where(upper, jnp.stack([other, grad_out]), jnp.stack([grad_out, other]))
    grads = gather(pair, ("y", "core"), 8)
    grads = grads.reshape(4, 2, 2, 2, 16, width).transpose(1, 3, 0, 2, 4, 5).reshape(512, width)

    z_hidden = gather(hidden, "z", 8).reshape(128, units)
    all_hidden = gather(z_hidden, "x", 4).reshape(512, units)

    scale_rows = jnp.repeat(weight_scales, BLOCK, axis=0)
    weight = (weight_values.astype(jnp.float32) * jnp.transpose(scale_rows)).astype(jnp.bfloat16)
    partial = lax.dot_general(
        grads, weight, (((1,), (1,)), ((), ())), preferred_element_type=jnp.float32
    ).astype(jnp.bfloat16)
    over_x = exchange(partial.reshape(4, 128, units), "x")
    over_x = over_x.astype(jnp.float32).sum(0).astype(jnp.bfloat16)
    over_z = exchange(over_x.reshape(8, 16, units), "z")
    hidden_grad = over_z.astype(jnp.float32).sum(0)

    weight_grad = lax.dot_general(
        all_hidden, grads, (((0,), (0,)), ((), ())), preferred_element_type=jnp.float32
    ).astype(jnp.bfloat16)
    gate_grad = (hidden_grad * up_f * sig * (1.0 + gate_f * (1.0 - sig))).astype(jnp.bfloat16)
    up_grad = (hidden_grad * act).astype(jnp.bfloat16)
    return (weight_grad, gate_grad, up_grad)


def solution(mesh):
    fine = Mesh(mesh.devices.reshape(4, 2, 2, 8, 4), ("y", "zh", "core", "z", "x"))
    row, col = ("y", "zh", "core"), ("z", "x")
    placed = (P(row, col), P(col, row), P(col, row), P(row, col), P(col, row))
    return jax.shard_map(
        per_device,
        mesh=fine,
        in_specs=placed,
        out_specs=(P(row, col), P(col, row), P(col, row)),
        check_vma=False,
    )
```

time: 545 us -> 150 us (0.28)
  the two profiles are of different devices: /device:TPU:2 before, /device:TPU:32 now
where the time goes in v1:
time: 150 us
  blocking collectives  109 us (73%)
  starting transfers between devices  19.3 us (13%)
  waiting for transfers between devices  8.61 us (6%)
  matrix products  4.85 us (3%)
  local copies, waits for them, and re-layouts  3.81 us (3%)
  other arithmetic  3.35 us (2%)
    all_to_all x4, blocking collectives, exchange(): return lax.all_to_all(parts, axes, split_axis=0, concat_axis=0)  109 us
    ppermute x1, starting transfers between devices, per_device(): other = lax.ppermute(grad_out, 'zh', [(0, 1), (1, 0)])  14.8 us
    all_to_all x1, waiting for transfers between devices, exchange(): return lax.all_to_all(parts, axes, split_axis=0, concat_axis=0)  6.07 us
    all_to_all x1, starting transfers between devices, exchange(): return lax.all_to_all(parts, axes, split_axis=0, concat_axis=0)  4.47 us
  transfers between devices with their start and end apart: 2, of which 2 were waited for; matrix products, arithmetic and copies ran while one was open for 3% of the time, Pallas kernels for 0%

profile of v1, /device:TPU:32, one launch (start us, length us, event | category | flops | bytes accessed | tf_op | source)
XLA Modules:
  0.0 149.6 jit_solution(15792220059262723933)
XLA Ops:
  0.6 14.8 %collective-permute-start = (bf16[32,512]{1,0:T(8,128)(2,1)}, bf16[32,512]{1,0:T(8,128)(2,1)S(1)}, u32[]{:S(2)}, u32[]{:S(2)}) collective-permute-start(bf16[32,512]{1,0:T(8,128)(2,1)} %param.5), channel_id=1, source_target_pairs={{0,64},{64,0},{1,65},{65,1},{2,66},{66,2},{3,67},{67,3},{4,68},{68... | collective-permute-start | bytes 98312 | tf_op jit(solution)/shard_map/ppermute | solution.py:26
  15.5 2.5 %collective-permute-done = bf16[32,512]{1,0:T(8,128)(2,1)S(1)} collective-permute-done((bf16[32,512]{1,0:T(8,128)(2,1)}, bf16[32,512]{1,0:T(8,128)(2,1)S(1)}, u32[]{:S(2)}, u32[]{:S(2)}) %collective-permute-start) | collective-permute-done | bytes 32800 | tf_op jit(solution)/shard_map/ppermute | solution.py:26
  18.0 0.8 maximum_select_fusion
  18.8 0.8 broadcast_in_dim.25
  19.7 4.5 %all-to-all-start.2 = ((bf16[8,2,32,512]{3,2,1,0:T(8,128)(2,1)}), bf16[8,2,32,512]{3,2,1,0:T(8,128)(2,1)S(1)}, u32[]{:S(2)}, u32[]{:S(2)}) async-start(bf16[8,2,32,512]{3,2,1,0:T(8,128)(2,1)} %broadcast_in_dim.25), calls=%async_computation.2 | async-start | bytes 1048576 | tf_op jit(solution)/shard_map/all_to_all | solution.py:10
  24.1 0.0 copy-start
  24.2 2.8 %copy.13 = bf16[1664,512]{0,1:T(8,128)(2,1)S(1)} copy(bf16[1664,512]{1,0:T(8,128)(2,1)} %param.8) | data formatting | bytes 3407872 | tf_op args[3]
  26.9 0.0 copy-done
  27.0 1.5 fusion
  28.4 6.1 %all-to-all-done.2 = bf16[8,2,32,512]{3,2,1,0:T(8,128)(2,1)S(1)} async-done(((bf16[8,2,32,512]{3,2,1,0:T(8,128)(2,1)}), bf16[8,2,32,512]{3,2,1,0:T(8,128)(2,1)S(1)}, u32[]{:S(2)}, u32[]{:S(2)}) %all-to-all-start.2) | async-done | bytes 524320 | tf_op jit(solution)/shard_map/all_to_all | solution.py:10
  34.5 2.6 %convolution_convert_fusion = bf16[512,1664]{1,0:T(8,128)(2,1)S(1)} fusion(bf16[512,512]{1,0:T(8,128)(2,1)S(1)} %bitcast.25, bf16[1664,512]{0,1:T(8,128)(2,1)} %fusion), kind=kOutput, calls=%fused_computation.2 | convolution fusion | flops 873267200 | bytes 3932160 | tf_op jit(solution)/shard_map/dot_general | solution.py:37
  37.1 26.0 %all_to_all.25 = bf16[4,128,1664]{2,1,0:T(8,128)(2,1)S(1)} all-to-all(bf16[4,128,1664]{2,1,0:T(8,128)(2,1)S(1)} %bitcast.22), channel_id=1, replica_groups=mesh['y'=4,'zh'=2,'core'=2,'z'=8,'x'=4] {'x'}, dimensions={0} | all-to-all | bytes 3407872 | tf_op jit(solution)/shard_map/all_to_all | solution.py:10
  63.1 0.0 copy-start.1
  63.1 0.0 copy-start.2
  63.1 0.3 reduce_sum.21
  63.4 31.2 %all_to_all.26 = bf16[8,16,1664]{2,1,0:T(8,128)(2,1)S(1)} all-to-all(bf16[8,16,1664]{2,1,0:T(8,128)(2,1)S(1)} %bitcast.23), channel_id=1, replica_groups=mesh['y'=4,'zh'=2,'core'=2,'z'=8,'x'=4] {'z'}, dimensions={0} | all-to-all | bytes 851968 | tf_op jit(solution)/shard_map/all_to_all | solution.py:10
  94.7 0.1 convert_reduce_fusion
  94.7 0.0 copy-done.1
  94.7 0.0 copy-done.2
  94.7 0.7 multiply_convert_fusion
  95.5 28.0 %all_to_all.27 = bf16[8,16,1664]{2,1,0:T(8,128)(2,1)S(1)} all-to-all(bf16[8,16,1664]{2,1,0:T(8,128)(2,1)S(1)} %broadcast_in_dim.10), channel_id=1, replica_groups=mesh['y'=4,'zh'=2,'core'=2,'z'=8,'x'=4] {'z'}, dimensions={0} | all-to-all | bytes 851968 | tf_op jit(solution)/shard_map/all_to_all | solution.py:10
  123.5 0.1 broadcast_in_dim.24
  123.6 23.7 %all_to_all.28 = bf16[4,128,1664]{2,1,0:T(8,128)(2,1)S(1)} all-to-all(bf16[4,128,1664]{2,1,0:T(8,128)(2,1)S(1)} %broadcast_in_dim.24), channel_id=1, replica_groups=mesh['y'=4,'zh'=2,'core'=2,'z'=8,'x'=4] {'x'}, dimensions={0} | all-to-all | bytes 3407872 | tf_op jit(solution)/shard_map/all_to_all | solution.py:10
  147.3 2.3 %convolution_convert_fusion.1 = bf16[1664,512]{1,0:T(8,128)(2,1)} fusion(bf16[512,1664]{1,0:T(8,128)(2,1)S(1)} %bitcast.21, bf16[512,512]{1,0:T(8,128)(2,1)S(1)} %bitcast.26), kind=kOutput, calls=%fused_computation.3 | convolution fusion | flops 873267200 | bytes 3932160 | tf_op jit(solution)/shard_map/dot_general | solution.py:45
  (2 shorter events, 0.1 us)
Async XLA Ops:
  0.6 17.4 %collective-permute-start = (bf16[32,512]{1,0:T(8,128)(2,1)}, bf16[32,512]{1,0:T(8,128)(2,1)S(1)}, u32[]{:S(2)}, u32[]{:S(2)}) collective-permute-start(bf16[32,512]{1,0:T(8,128)(2,1)} %param.5), channel_id=1, source_target_pairs={{0,64},{64,0},{1,65},{65,1},{2,66},{66,2},{3,67},{67,3},{4,68},{68... | collective-permute-start | bytes 98312 | tf_op jit(solution)/shard_map/ppermute | solution.py:26
  19.7 14.8 %all-to-all-start.2 = ((bf16[8,2,32,512]{3,2,1,0:T(8,128)(2,1)}), bf16[8,2,32,512]{3,2,1,0:T(8,128)(2,1)S(1)}, u32[]{:S(2)}, u32[]{:S(2)}) async-start(bf16[8,2,32,512]{3,2,1,0:T(8,128)(2,1)} %broadcast_in_dim.25), calls=%async_computation.2 | async-start | bytes 1048576 | tf_op jit(solution)/shard_map/all_to_all | solution.py:10
  24.1 2.8 %copy-start = (f32[16,1664]{1,0:T(8,128)S(1)}, f32[16,1664]{1,0:T(8,128)}, u32[]{:S(2)}) copy-start(f32[16,1664]{1,0:T(8,128)} %param.9) | copy-start | bytes 319492
  63.1 31.6 %copy-start.1 = (bf16[16,1664]{1,0:T(8,128)(2,1)S(1)}, bf16[16,1664]{1,0:T(8,128)(2,1)}, u32[]{:S(2)}) copy-start(bf16[16,1664]{1,0:T(8,128)(2,1)} %param.6) | copy-start | bytes 159748
  63.1 31.6 %copy-start.2 = (bf16[16,1664]{1,0:T(8,128)(2,1)S(1)}, bf16[16,1664]{1,0:T(8,128)(2,1)}, u32[]{:S(2)}) copy-start(bf16[16,1664]{1,0:T(8,128)(2,1)} %param.7) | copy-start | bytes 159748

commit v2 on v1

v2 whole, which is shorter than its diff:
```python
import jax
import jax.numpy as jnp
from jax import lax
from jax.sharding import Mesh, PartitionSpec as P

BLOCK = 32


def exchange(parts, axes):
    return lax.all_to_all(parts, axes, split_axis=0, concat_axis=0)


def swap(block, axis, size, stride):
    return lax.ppermute(block, axis, [(i, i ^ stride) for i in range(size)])


def shift(block, k):
    return lax.ppermute(block, "x", [(i, (i + k) % 4) for i in range(4)])


def in_order(mine, other, upper, axis):
    return jnp.where(upper, jnp.stack([other, mine], axis), jnp.stack([mine, other], axis))


def per_device(grad_out, gate_pre, up_pre, weight_values, weight_scales):
    units = gate_pre.shape[1]
    width = grad_out.shape[1]
    gate_f = gate_pre.astype(jnp.float32)
    up_f = up_pre.astype(jnp.float32)
    sig = jax.nn.sigmoid(gate_f)
    act = gate_f * sig
    hidden = (act * up_f).astype(jnp.bfloat16)
    zb, x = lax.axis_index("zb"), lax.axis_index("x")

    part = exchange(jnp.broadcast_to(hidden[None], (4,) + hidden.shape), "za")
    pair = in_order(grad_out, swap(grad_out, "zh", 2, 1), lax.axis_index("zh") == 1, 0)
    spread = (jnp.arange(width)[None] // BLOCK == jnp.arange(width // BLOCK)[:, None]).astype(jnp.float32)
    scale = lax.dot_general(weight_scales, spread, (((0,), (0,)), ((), ())), preferred_element_type=jnp.float32)
    weight = (weight_values.astype(jnp.float32) * scale).astype(jnp.bfloat16)
    pair, part, weight = lax.optimization_barrier((pair, part, weight))

    mine = in_order(part, swap(part, "zb", 2, 1), zb == 1, 1).reshape(128, units)
    grads = exchange(jnp.broadcast_to(pair[None], (8,) + pair.shape), ("y", "core"))
    grads = grads.reshape(4, 2, 2, 2, 16, width)
    by_part = grads.transpose(2, 1, 3, 0, 4, 5).reshape(512, width)
    by_x = grads.transpose(1, 3, 0, 2, 4, 5).reshape(4, 128, width)
    partial = lax.dot_general(
        by_part, weight, (((1,), (1,)), ((), ())), preferred_element_type=jnp.float32
    ).astype(jnp.bfloat16)
    partial, mine = lax.optimization_barrier((partial, mine))

    over_x = exchange(partial.reshape(8, 64, units), ("zb", "x"))
    next_x = shift(mine, 3)
    last_x = shift(mine, 1)
    far_x = shift(mine, 2)
    over_x = over_x.astype(jnp.float32).sum(0).astype(jnp.bfloat16)
    over_z = exchange(over_x.reshape(4, 16, units), "za")
    hidden_grad = over_z.astype(jnp.float32).sum(0)

    all_hidden = jnp.concatenate([mine, next_x, far_x, last_x])
    rolled = lax.dynamic_slice_in_dim(jnp.concatenate([by_x, by_x]), x, 4).reshape(512, width)
    weight_grad = lax.dot_general(
        all_hidden, rolled, (((0,), (0,)), ((), ())), preferred_element_type=jnp.float32
    ).astype(jnp.bfloat16)
    gate_grad = (hidden_grad * up_f * sig * (1.0 + gate_f * (1.0 - sig))).astype(jnp.bfloat16)
    up_grad = (hidden_grad * act).astype(jnp.bfloat16)
    return (weight_grad, gate_grad, up_grad)


def solution(mesh):
    fine = Mesh(mesh.devices.reshape(4, 2, 2, 4, 2, 4), ("y", "zh", "core", "za", "zb", "x"))
    row, col = ("y", "zh", "core"), ("za", "zb", "x")
    placed = (P(row, col), P(col, row), P(col, row), P(row, col), P(col, row))
    return jax.shard_map(
        per_device,
        mesh=fine,
        in_specs=placed,
        out_specs=(P(row, col), P(col, row), P(col, row)),
        check_vma=False,
    )
```

time: 150 us -> 104 us (0.69)
  the two profiles are of different devices: /device:TPU:32 before, /device:TPU:2 now
where the time goes in v2:
time: 104 us; the launch traced here: 103 us
  starting transfers between devices  55.3 us (53%)
  waiting for transfers between devices  32.3 us (31%)
  matrix products  7.62 us (7%)
  local copies, waits for them, and re-layouts  4.42 us (4%)
  other arithmetic  2.89 us (3%)
    all_to_all x4, starting transfers between devices, exchange(): return lax.all_to_all(parts, axes, split_axis=0, concat_axis=0)  31.3 us
    all_to_all x4, waiting for transfers between devices, exchange(): return lax.all_to_all(parts, axes, split_axis=0, concat_axis=0)  25.2 us
    ppermute x2, starting transfers between devices, swap(): return lax.ppermute(block, axis, [(i, i ^ stride) for i in range(size)])  13.6 us
    ppermute x3, starting transfers between devices, shift(): return lax.ppermute(block, 'x', [(i, (i + k) % 4) for i in range(4)])  10.4 us
    ppermute x2, waiting for transfers between devices, swap(): return lax.ppermute(block, axis, [(i, i ^ stride) for i in range(size)])  7.07 us
    dot_general x1, matrix products, per_device(): lax.dot_general(all_hidden, rolled, (((0,), (0,)), ((), ())), preferred_e...  3.45 us
    unnamed x11, local copies, waits for them, and re-layouts  2.78 us
    dot_general x1, matrix products, per_device(): lax.dot_general(by_part, weight, (((1,), (1,)), ((), ())), preferred_elem...  2.32 us
  transfers between devices with their start and end apart: 9, of which 4 were waited for; matrix products, arithmetic and copies ran while one was open for 9% of the time, Pallas kernels for 0%

profile of v2, /device:TPU:2, one launch (start us, length us, event | category | flops | bytes accessed | tf_op | source)
XLA Modules:
  0.0 103.4 jit_solution(4942111567217398783)
XLA Ops:
  0.6 0.0 copy-start
  0.6 0.9 fusion.9
  1.6 0.7 broadcast_in_dim.4
  2.3 11.2 %all-to-all-start = ((bf16[4,16,1664]{2,1,0:T(8,128)(2,1)}), bf16[4,16,1664]{2,1,0:T(8,128)(2,1)S(1)}, u32[]{:S(2)}, u32[]{:S(2)}) async-start(bf16[4,16,1664]{2,1,0:T(8,128)(2,1)} %broadcast_in_dim.4), calls=%async_computation | async-start | bytes 425984 | tf_op jit(solution)/shard_map/all_to_all | solution.py:10
  13.4 9.1 %collective-permute-start = (bf16[32,512]{1,0:T(8,128)(2,1)}, bf16[32,512]{1,0:T(8,128)(2,1)S(1)}, u32[]{:S(2)}, u32[]{:S(2)}) collective-permute-start(bf16[32,512]{1,0:T(8,128)(2,1)} %param.5), channel_id=1, source_target_pairs={{0,64},{64,0},{1,65},{65,1},{2,66},{66,2},{3,67},{67,3},{4,68},{68... | collective-permute-start | bytes 98312 | tf_op jit(solution)/shard_map/ppermute | solution.py:14
  22.6 2.8 %copy.14 = bf16[1664,512]{0,1:T(8,128)(2,1)S(1)} copy(bf16[1664,512]{1,0:T(8,128)(2,1)} %param.8) | data formatting | bytes 3407872 | tf_op args[3]
  25.3 0.0 copy-start.4
  25.3 1.9 %fusion = bf16[1664,512]{0,1:T(8,128)(2,1)} fusion(bf16[1664,512]{0,1:T(8,128)(2,1)S(1)} %copy.14, f32[16,1664]{1,0:T(8,128)S(1)} %copy-done, s32[512]{0:T(512)S(1)} %add_select_fusion), kind=kOutput, calls=%fused_computation.1 | convolution fusion | flops 29827072 | bytes 3516416 | tf_op jit(solution)/shard_map/dot_general | solution.py:38
  27.2 1.2 %collective-permute-done = bf16[32,512]{1,0:T(8,128)(2,1)S(1)} collective-permute-done((bf16[32,512]{1,0:T(8,128)(2,1)}, bf16[32,512]{1,0:T(8,128)(2,1)S(1)}, u32[]{:S(2)}, u32[]{:S(2)}) %collective-permute-start) | collective-permute-done | bytes 32800 | tf_op jit(solution)/shard_map/ppermute | solution.py:14
  28.4 0.0 copy-start.1
  28.4 0.0 all-to-all-done
  28.4 0.8 broadcast_in_dim.5
  29.3 4.5 %all-to-all-start.1 = ((bf16[8,2,32,512]{3,2,1,0:T(8,128)(2,1)}), bf16[8,2,32,512]{3,2,1,0:T(8,128)(2,1)S(1)}, u32[]{:S(2)}, u32[]{:S(2)}) async-start(bf16[8,2,32,512]{3,2,1,0:T(8,128)(2,1)} %broadcast_in_dim.5), calls=%async_computation.1 | async-start | bytes 1048576 | tf_op jit(solution)/shard_map/all_to_all | solution.py:10
  33.7 4.5 %collective-permute-start.1 = (bf16[4,16,1664]{2,1,0:T(8,128)(2,1)S(1)}, bf16[4,16,1664]{2,1,0:T(8,128)(2,1)S(1)}, u32[]{:S(2)}, u32[]{:S(2)}) collective-permute-start(bf16[4,16,1664]{2,1,0:T(8,128)(2,1)S(1)} %all-to-all-done), channel_id=1, source_target_pairs={{0,4},{4,0},{1,5},{5,1},{2,6},{6,2},{3,7},{7,3},{8,12},{12,8},{9,1... | collective-permute-start | bytes 638984 | tf_op jit(solution)/shard_map/ppermute | solution.py:14
  38.2 5.9 %collective-permute-done.1 = bf16[4,16,1664]{2,1,0:T(8,128)(2,1)S(1)} collective-permute-done((bf16[4,16,1664]{2,1,0:T(8,128)(2,1)S(1)}, bf16[4,16,1664]{2,1,0:T(8,128)(2,1)S(1)}, u32[]{:S(2)}, u32[]{:S(2)}) %collective-permute-start.1) | collective-permute-done | bytes 213024 | tf_op jit(solution)/shard_map/ppermute | solution.py:14
  44.1 0.1 maximum_select_fusion
  44.2 0.0 all-to-all-done.1
  44.3 2.3 %convolution_convert_fusion.1 = bf16[512,1664]{1,0:T(8,128)(2,1)} fusion(bf16[512,512]{1,0:T(8,128)(2,1)S(1)} %bitcast.28, bf16[1664,512]{0,1:T(8,128)(2,1)S(1)} %copy-done.1), kind=kOutput, calls=%fused_computation.3 | convolution fusion | flops 873267200 | bytes 3932160 | tf_op jit(solution)/shard_map/dot_general | solution.py:47
  46.6 6.7 %all-to-all-start.2 = ((bf16[8,64,1664]{2,1,0:T(8,128)(2,1)}), bf16[8,64,1664]{2,1,0:T(8,128)(2,1)S(1)}, u32[]{:S(2)}, u32[]{:S(2)}) async-start(bf16[8,64,1664]{2,1,0:T(8,128)(2,1)} %bitcast.26), calls=%async_computation.2 | async-start | bytes 3407872 | tf_op jit(solution)/shard_map/all_to_all | solution.py:10
  53.3 3.4 %collective-permute-start.4 = (bf16[128,1664]{1,0:T(8,128)(2,1)S(1)}, bf16[128,1664]{1,0:T(8,128)(2,1)S(1)}, u32[]{:S(2)}, u32[]{:S(2)}) collective-permute-start(bf16[128,1664]{1,0:T(8,128)(2,1)S(1)} %bitcast.30), channel_id=1, source_target_pairs={{0,1},{1,2},{2,3},{3,0},{4,5},{5,6},{6,7},{7,4},{8,9},{9,10},{10,1... | collective-permute-start | bytes 1277960 | tf_op jit(solution)/shard_map/ppermute | solution.py:18
  56.7 2.5 %collective-permute-start.3 = (bf16[128,1664]{1,0:T(8,128)(2,1)S(1)}, bf16[128,1664]{1,0:T(8,128)(2,1)}, u32[]{:S(2)}, u32[]{:S(2)}) collective-permute-start(bf16[128,1664]{1,0:T(8,128)(2,1)S(1)} %bitcast.31), channel_id=1, source_target_pairs={{0,2},{1,3},{2,0},{3,1},{4,6},{5,7},{6,4},{7,5},{8,10},{9,11},{10,... | collective-permute-start | bytes 1277960 | tf_op jit(solution)/shard_map/ppermute | solution.py:18
  59.2 4.5 %collective-permute-start.2 = (bf16[128,1664]{1,0:T(8,128)(2,1)S(1)}, bf16[128,1664]{1,0:T(8,128)(2,1)}, u32[]{:S(2)}, u32[]{:S(2)}) collective-permute-start(bf16[128,1664]{1,0:T(8,128)(2,1)S(1)} %bitcast.32), channel_id=1, source_target_pairs={{0,3},{1,0},{2,1},{3,2},{4,7},{5,4},{6,5},{7,6},{8,11},{9,8},{10,9... | collective-permute-start | bytes 1277960 | tf_op jit(solution)/shard_map/ppermute | solution.py:18
  63.8 18.9 %all-to-all-done.2 = bf16[8,64,1664]{2,1,0:T(8,128)(2,1)S(1)} async-done(((bf16[8,64,1664]{2,1,0:T(8,128)(2,1)}), bf16[8,64,1664]{2,1,0:T(8,128)(2,1)S(1)}, u32[]{:S(2)}, u32[]{:S(2)}) %all-to-all-start.2) | async-done | bytes 1703968 | tf_op jit(solution)/shard_map/all_to_all | solution.py:10
  82.7 1.0 reduce_sum.21
  83.7 8.9 %all-to-all-start.3 = ((bf16[4,16,1664]{2,1,0:T(8,128)(2,1)}), bf16[4,16,1664]{2,1,0:T(8,128)(2,1)S(1)}, u32[]{:S(2)}, u32[]{:S(2)}) async-start(bf16[4,16,1664]{2,1,0:T(8,128)(2,1)} %bitcast.13), calls=%async_computation.3 | async-start | bytes 425984 | tf_op jit(solution)/shard_map/all_to_all | solution.py:10
  92.7 0.2 fusion.8
  92.9 0.0 collective-permute-done.3
  92.9 0.0 copy-start.2
  92.9 0.0 copy-start.3
  92.9 3.5 %convolution_convert_fusion = bf16[1664,512]{1,0:T(8,128)(2,1)} fusion(bf16[512,512]{1,0:T(8,128)(2,1)S(1)} %bitcast.29, bf16[128,1664]{1,0:T(8,128)(2,1)S(1)} %collective-permute-done.4, bf16[128,1664]{1,0:T(8,128)(2,1)} %collective-permute-done.3, bf16[128,1664]{1,0:T(8,128)(2,1)} %collective-permute-done.2, bf16[128,1664]{1,0:T(8,128)(2,1)S(1)} %bitcast.33), kind=kOutput, calls=%fused_computation.2 | convolution fusion | flops 880082944 | bytes 3932160 | tf_op jit(solution)/shard_map/dot_general | solution.py:62
  96.4 6.3 %all-to-all-done.3 = bf16[4,16,1664]{2,1,0:T(8,128)(2,1)S(1)} async-done(((bf16[4,16,1664]{2,1,0:T(8,128)(2,1)}), bf16[4,16,1664]{2,1,0:T(8,128)(2,1)S(1)}, u32[]{:S(2)}, u32[]{:S(2)}) %all-to-all-start.3) | async-done | bytes 213024 | tf_op jit(solution)/shard_map/all_to_all | solution.py:10
  102.7 0.7 multiply_convert_fusion
  (12 shorter events, 0.1 us)
Async XLA Ops:
  0.6 24.7 %copy-start = (f32[16,1664]{1,0:T(8,128)S(1)}, f32[16,1664]{1,0:T(8,128)}, u32[]{:S(2)}) copy-start(f32[16,1664]{1,0:T(8,128)} %param.9) | copy-start | bytes 319492
  2.3 26.1 %all-to-all-start = ((bf16[4,16,1664]{2,1,0:T(8,128)(2,1)}), bf16[4,16,1664]{2,1,0:T(8,128)(2,1)S(1)}, u32[]{:S(2)}, u32[]{:S(2)}) async-start(bf16[4,16,1664]{2,1,0:T(8,128)(2,1)} %broadcast_in_dim.4), calls=%async_computation | async-start | bytes 425984 | tf_op jit(solution)/shard_map/all_to_all | solution.py:10
  13.4 14.9 %collective-permute-start = (bf16[32,512]{1,0:T(8,128)(2,1)}, bf16[32,512]{1,0:T(8,128)(2,1)S(1)}, u32[]{:S(2)}, u32[]{:S(2)}) collective-permute-start(bf16[32,512]{1,0:T(8,128)(2,1)} %param.5), channel_id=1, source_target_pairs={{0,64},{64,0},{1,65},{65,1},{2,66},{66,2},{3,67},{67,3},{4,68},{68... | collective-permute-start | bytes 98312 | tf_op jit(solution)/shard_map/ppermute | solution.py:14
  25.3 3.0 %copy-start.4 = (bf16[32,512]{1,0:T(8,128)(2,1)S(1)}, bf16[32,512]{1,0:T(8,128)(2,1)}, u32[]{:S(2)}) copy-start(bf16[32,512]{1,0:T(8,128)(2,1)} %param.5) | copy-start | bytes 98308
  28.4 15.9 %copy-start.1 = (bf16[1664,512]{0,1:T(8,128)(2,1)S(1)}, bf16[1664,512]{0,1:T(8,128)(2,1)}, u32[]{:S(2)}) copy-start(bf16[1664,512]{0,1:T(8,128)(2,1)} %fusion) | copy-start | bytes 5111812
  29.3 14.9 %all-to-all-start.1 = ((bf16[8,2,32,512]{3,2,1,0:T(8,128)(2,1)}), bf16[8,2,32,512]{3,2,1,0:T(8,128)(2,1)S(1)}, u32[]{:S(2)}, u32[]{:S(2)}) async-start(bf16[8,2,32,512]{3,2,1,0:T(8,128)(2,1)} %broadcast_in_dim.5), calls=%async_computation.1 | async-start | bytes 1048576 | tf_op jit(solution)/shard_map/all_to_all | solution.py:10
  33.7 10.4 %collective-permute-start.1 = (bf16[4,16,1664]{2,1,0:T(8,128)(2,1)S(1)}, bf16[4,16,1664]{2,1,0:T(8,128)(2,1)S(1)}, u32[]{:S(2)}, u32[]{:S(2)}) collective-permute-start(bf16[4,16,1664]{2,1,0:T(8,128)(2,1)S(1)} %all-to-all-done), channel_id=1, source_target_pairs={{0,4},{4,0},{1,5},{5,1},{2,6},{6,2},{3,7},{7,3},{8,12},{12,8},{9,1... | collective-permute-start | bytes 638984 | tf_op jit(solution)/shard_map/ppermute | solution.py:14
  46.6 36.1 %all-to-all-start.2 = ((bf16[8,64,1664]{2,1,0:T(8,128)(2,1)}), bf16[8,64,1664]{2,1,0:T(8,128)(2,1)S(1)}, u32[]{:S(2)}, u32[]{:S(2)}) async-start(bf16[8,64,1664]{2,1,0:T(8,128)(2,1)} %bitcast.26), calls=%async_computation.2 | async-start | bytes 3407872 | tf_op jit(solution)/shard_map/all_to_all | solution.py:10
  53.3 39.6 %collective-permute-start.4 = (bf16[128,1664]{1,0:T(8,128)(2,1)S(1)}, bf16[128,1664]{1,0:T(8,128)(2,1)S(1)}, u32[]{:S(2)}, u32[]{:S(2)}) collective-permute-start(bf16[128,1664]{1,0:T(8,128)(2,1)S(1)} %bitcast.30), channel_id=1, source_target_pairs={{0,1},{1,2},{2,3},{3,0},{4,5},{5,6},{6,7},{7,4},{8,9},{9,10},{10,1... | collective-permute-start | bytes 1277960 | tf_op jit(solution)/shard_map/ppermute | solution.py:18
  56.7 36.2 %collective-permute-start.3 = (bf16[128,1664]{1,0:T(8,128)(2,1)S(1)}, bf16[128,1664]{1,0:T(8,128)(2,1)}, u32[]{:S(2)}, u32[]{:S(2)}) collective-permute-start(bf16[128,1664]{1,0:T(8,128)(2,1)S(1)} %bitcast.31), channel_id=1, source_target_pairs={{0,2},{1,3},{2,0},{3,1},{4,6},{5,7},{6,4},{7,5},{8,10},{9,11},{10,... | collective-permute-start | bytes 1277960 | tf_op jit(solution)/shard_map/ppermute | solution.py:18
  59.2 33.7 %collective-permute-start.2 = (bf16[128,1664]{1,0:T(8,128)(2,1)S(1)}, bf16[128,1664]{1,0:T(8,128)(2,1)}, u32[]{:S(2)}, u32[]{:S(2)}) collective-permute-start(bf16[128,1664]{1,0:T(8,128)(2,1)S(1)} %bitcast.32), channel_id=1, source_target_pairs={{0,3},{1,0},{2,1},{3,2},{4,7},{5,4},{6,5},{7,6},{8,11},{9,8},{10,9... | collective-permute-start | bytes 1277960 | tf_op jit(solution)/shard_map/ppermute | solution.py:18
  83.7 19.0 %all-to-all-start.3 = ((bf16[4,16,1664]{2,1,0:T(8,128)(2,1)}), bf16[4,16,1664]{2,1,0:T(8,128)(2,1)S(1)}, u32[]{:S(2)}, u32[]{:S(2)}) async-start(bf16[4,16,1664]{2,1,0:T(8,128)(2,1)} %bitcast.13), calls=%async_computation.3 | async-start | bytes 425984 | tf_op jit(solution)/shard_map/all_to_all | solution.py:10
  92.9 9.8 %copy-start.2 = (bf16[16,1664]{1,0:T(8,128)(2,1)S(1)}, bf16[16,1664]{1,0:T(8,128)(2,1)}, u32[]{:S(2)}) copy-start(bf16[16,1664]{1,0:T(8,128)(2,1)} %param.7) | copy-start | bytes 159748
  92.9 9.8 %copy-start.3 = (bf16[16,1664]{1,0:T(8,128)(2,1)S(1)}, bf16[16,1664]{1,0:T(8,128)(2,1)}, u32[]{:S(2)}) copy-start(bf16[16,1664]{1,0:T(8,128)(2,1)} %param.6) | copy-start | bytes 159748

commit v3 on v2

--- a/solution.py
+++ b/solution.py
@@ -42,14 +42,14 @@
     mine = in_order(part, swap(part, "zb", 2, 1), zb == 1, 1).reshape(128, units)
     grads = exchange(jnp.broadcast_to(pair[None], (8,) + pair.shape), ("y", "core"))
     grads = grads.reshape(4, 2, 2, 2, 16, width)
-    by_part = grads.transpose(2, 1, 3, 0, 4, 5).reshape(512, width)
+    by_part = grads.transpose(1, 3, 2, 0, 4, 5).reshape(512, width)
     by_x = grads.transpose(1, 3, 0, 2, 4, 5).reshape(4, 128, width)
     partial = lax.dot_general(
         by_part, weight, (((1,), (1,)), ((), ())), preferred_element_type=jnp.float32
     ).astype(jnp.bfloat16)
     partial, mine = lax.optimization_barrier((partial, mine))
 
-    over_x = exchange(partial.reshape(8, 64, units), ("zb", "x"))
+    over_x = exchange(partial.reshape(8, 64, units), ("x", "zb"))
     next_x = shift(mine, 3)
     last_x = shift(mine, 1)
     far_x = shift(mine, 2)

time: 104 us -> 100 us (0.962)
  waiting for transfers between devices: 32.3 us -> 28.7 us
    all_to_all x4, waiting for transfers between devices: 25.2 us -> 15.6 us  [exchange(): return lax.all_to_all(parts, axes, split_axis=0, concat_axis=0)]
    ppermute x3, waiting for transfers between devices: 0.01 us -> 6.01 us  [shift(): return lax.ppermute(block, 'x', [(i, (i + k) % 4) for i in range(4)])]
  transfers between devices with their start and end apart: 9 -> 9, of which waited for: 4 -> 5; matrix products, arithmetic and copies ran while one was open for 9% -> 9% of each run, Pallas kernels for 0% -> 0%
where the time goes in v3:
time: 100 us; the launch traced here: 99.8 us
  starting transfers between devices  55.3 us (55%)
  waiting for transfers between devices  28.7 us (29%)
  matrix products  7.61 us (8%)
  local copies, waits for them, and re-layouts  4.41 us (4%)
  other arithmetic  2.89 us (3%)
    all_to_all x4, starting transfers between devices, exchange(): return lax.all_to_all(parts, axes, split_axis=0, concat_axis=0)  31.3 us
    all_to_all x4, waiting for transfers between devices, exchange(): return lax.all_to_all(parts, axes, split_axis=0, concat_axis=0)  15.6 us
    ppermute x2, starting transfers between devices, swap(): return lax.ppermute(block, axis, [(i, i ^ stride) for i in range(size)])  13.6 us
    ppermute x3, starting transfers between devices, shift(): return lax.ppermute(block, 'x', [(i, (i + k) % 4) for i in range(4)])  10.4 us
    ppermute x2, waiting for transfers between devices, swap(): return lax.ppermute(block, axis, [(i, i ^ stride) for i in range(size)])  7.07 us
    ppermute x3, waiting for transfers between devices, shift(): return lax.ppermute(block, 'x', [(i, (i + k) % 4) for i in range(4)])  6.01 us
    dot_general x1, matrix products, per_device(): lax.dot_general(all_hidden, rolled, (((0,), (0,)), ((), ())), preferred_e...  3.43 us
    unnamed x11, local copies, waits for them, and re-layouts  2.78 us
  transfers between devices with their start and end apart: 9, of which 5 were waited for; matrix products, arithmetic and copies ran while one was open for 9% of the time, Pallas kernels for 0%

profile of v3, /device:TPU:2, one launch (start us, length us, event | category | flops | bytes accessed | tf_op | source)
XLA Modules:
  0.0 99.8 jit_solution(15929846933566850997)
XLA Ops:
  0.6 0.0 copy-start
  0.6 0.9 fusion.9
  1.6 0.7 broadcast_in_dim.4
  2.3 11.2 %all-to-all-start = ((bf16[4,16,1664]{2,1,0:T(8,128)(2,1)}), bf16[4,16,1664]{2,1,0:T(8,128)(2,1)S(1)}, u32[]{:S(2)}, u32[]{:S(2)}) async-start(bf16[4,16,1664]{2,1,0:T(8,128)(2,1)} %broadcast_in_dim.4), calls=%async_computation | async-start | bytes 425984 | tf_op jit(solution)/shard_map/all_to_all | solution.py:10
  13.4 9.1 %collective-permute-start = (bf16[32,512]{1,0:T(8,128)(2,1)}, bf16[32,512]{1,0:T(8,128)(2,1)S(1)}, u32[]{:S(2)}, u32[]{:S(2)}) collective-permute-start(bf16[32,512]{1,0:T(8,128)(2,1)} %param.5), channel_id=1, source_target_pairs={{0,64},{64,0},{1,65},{65,1},{2,66},{66,2},{3,67},{67,3},{4,68},{68... | collective-permute-start | bytes 98312 | tf_op jit(solution)/shard_map/ppermute | solution.py:14
  22.6 2.8 %copy.14 = bf16[1664,512]{0,1:T(8,128)(2,1)S(1)} copy(bf16[1664,512]{1,0:T(8,128)(2,1)} %param.8) | data formatting | bytes 3407872 | tf_op args[3]
  25.3 0.0 copy-start.4
  25.3 1.9 %fusion = bf16[1664,512]{0,1:T(8,128)(2,1)} fusion(bf16[1664,512]{0,1:T(8,128)(2,1)S(1)} %copy.14, f32[16,1664]{1,0:T(8,128)S(1)} %copy-done, s32[512]{0:T(512)S(1)} %add_select_fusion), kind=kOutput, calls=%fused_computation.1 | convolution fusion | flops 29827072 | bytes 3516416 | tf_op jit(solution)/shard_map/dot_general | solution.py:38
  27.2 1.2 %collective-permute-done = bf16[32,512]{1,0:T(8,128)(2,1)S(1)} collective-permute-done((bf16[32,512]{1,0:T(8,128)(2,1)}, bf16[32,512]{1,0:T(8,128)(2,1)S(1)}, u32[]{:S(2)}, u32[]{:S(2)}) %collective-permute-start) | collective-permute-done | bytes 32800 | tf_op jit(solution)/shard_map/ppermute | solution.py:14
  28.4 0.0 copy-start.1
  28.4 0.0 all-to-all-done
  28.4 0.8 broadcast_in_dim.5
  29.3 4.5 %all-to-all-start.1 = ((bf16[8,2,32,512]{3,2,1,0:T(8,128)(2,1)}), bf16[8,2,32,512]{3,2,1,0:T(8,128)(2,1)S(1)}, u32[]{:S(2)}, u32[]{:S(2)}) async-start(bf16[8,2,32,512]{3,2,1,0:T(8,128)(2,1)} %broadcast_in_dim.5), calls=%async_computation.1 | async-start | bytes 1048576 | tf_op jit(solution)/shard_map/all_to_all | solution.py:10
  33.7 4.5 %collective-permute-start.1 = (bf16[4,16,1664]{2,1,0:T(8,128)(2,1)S(1)}, bf16[4,16,1664]{2,1,0:T(8,128)(2,1)S(1)}, u32[]{:S(2)}, u32[]{:S(2)}) collective-permute-start(bf16[4,16,1664]{2,1,0:T(8,128)(2,1)S(1)} %all-to-all-done), channel_id=1, source_target_pairs={{0,4},{4,0},{1,5},{5,1},{2,6},{6,2},{3,7},{7,3},{8,12},{12,8},{9,1... | collective-permute-start | bytes 638984 | tf_op jit(solution)/shard_map/ppermute | solution.py:14
  38.2 5.9 %collective-permute-done.1 = bf16[4,16,1664]{2,1,0:T(8,128)(2,1)S(1)} collective-permute-done((bf16[4,16,1664]{2,1,0:T(8,128)(2,1)S(1)}, bf16[4,16,1664]{2,1,0:T(8,128)(2,1)S(1)}, u32[]{:S(2)}, u32[]{:S(2)}) %collective-permute-start.1) | collective-permute-done | bytes 213024 | tf_op jit(solution)/shard_map/ppermute | solution.py:14
  44.1 0.1 maximum_select_fusion
  44.2 0.0 all-to-all-done.1
  44.3 2.3 %convolution_convert_fusion.1 = bf16[512,1664]{1,0:T(8,128)(2,1)} fusion(bf16[512,512]{1,0:T(8,128)(2,1)S(1)} %bitcast.28, bf16[1664,512]{0,1:T(8,128)(2,1)S(1)} %copy-done.1), kind=kOutput, calls=%fused_computation.3 | convolution fusion | flops 873267200 | bytes 3932160 | tf_op jit(solution)/shard_map/dot_general | solution.py:47
  46.6 6.7 %all-to-all-start.2 = ((bf16[8,64,1664]{2,1,0:T(8,128)(2,1)}), bf16[8,64,1664]{2,1,0:T(8,128)(2,1)S(1)}, u32[]{:S(2)}, u32[]{:S(2)}) async-start(bf16[8,64,1664]{2,1,0:T(8,128)(2,1)} %bitcast.26), calls=%async_computation.2 | async-start | bytes 3407872 | tf_op jit(solution)/shard_map/all_to_all | solution.py:10
  53.3 3.4 %collective-permute-start.4 = (bf16[128,1664]{1,0:T(8,128)(2,1)S(1)}, bf16[128,1664]{1,0:T(8,128)(2,1)S(1)}, u32[]{:S(2)}, u32[]{:S(2)}) collective-permute-start(bf16[128,1664]{1,0:T(8,128)(2,1)S(1)} %bitcast.30), channel_id=1, source_target_pairs={{0,1},{1,2},{2,3},{3,0},{4,5},{5,6},{6,7},{7,4},{8,9},{9,10},{10,1... | collective-permute-start | bytes 1277960 | tf_op jit(solution)/shard_map/ppermute | solution.py:18
  56.7 2.5 %collective-permute-start.3 = (bf16[128,1664]{1,0:T(8,128)(2,1)S(1)}, bf16[128,1664]{1,0:T(8,128)(2,1)}, u32[]{:S(2)}, u32[]{:S(2)}) collective-permute-start(bf16[128,1664]{1,0:T(8,128)(2,1)S(1)} %bitcast.31), channel_id=1, source_target_pairs={{0,2},{1,3},{2,0},{3,1},{4,6},{5,7},{6,4},{7,5},{8,10},{9,11},{10,... | collective-permute-start | bytes 1277960 | tf_op jit(solution)/shard_map/ppermute | solution.py:18
  59.2 4.5 %collective-permute-start.2 = (bf16[128,1664]{1,0:T(8,128)(2,1)S(1)}, bf16[128,1664]{1,0:T(8,128)(2,1)}, u32[]{:S(2)}, u32[]{:S(2)}) collective-permute-start(bf16[128,1664]{1,0:T(8,128)(2,1)S(1)} %bitcast.32), channel_id=1, source_target_pairs={{0,3},{1,0},{2,1},{3,2},{4,7},{5,4},{6,5},{7,6},{8,11},{9,8},{10,9... | collective-permute-start | bytes 1277960 | tf_op jit(solution)/shard_map/ppermute | solution.py:18
  63.8 11.7 %all-to-all-done.2 = bf16[8,64,1664]{2,1,0:T(8,128)(2,1)S(1)} async-done(((bf16[8,64,1664]{2,1,0:T(8,128)(2,1)}), bf16[8,64,1664]{2,1,0:T(8,128)(2,1)S(1)}, u32[]{:S(2)}, u32[]{:S(2)}) %all-to-all-start.2) | async-done | bytes 1703968 | tf_op jit(solution)/shard_map/all_to_all | solution.py:10
  75.5 1.0 reduce_sum.21
  76.5 8.9 %all-to-all-start.3 = ((bf16[4,16,1664]{2,1,0:T(8,128)(2,1)}), bf16[4,16,1664]{2,1,0:T(8,128)(2,1)S(1)}, u32[]{:S(2)}, u32[]{:S(2)}) async-start(bf16[4,16,1664]{2,1,0:T(8,128)(2,1)} %bitcast.13), calls=%async_computation.3 | async-start | bytes 425984 | tf_op jit(solution)/shard_map/all_to_all | solution.py:10
  85.5 0.2 fusion.8
  85.7 0.0 collective-permute-done.4
  85.7 0.0 collective-permute-done.3
  85.7 6.0 %collective-permute-done.2 = bf16[128,1664]{1,0:T(8,128)(2,1)} collective-permute-done((bf16[128,1664]{1,0:T(8,128)(2,1)S(1)}, bf16[128,1664]{1,0:T(8,128)(2,1)}, u32[]{:S(2)}, u32[]{:S(2)}) %collective-permute-start.2) | collective-permute-done | bytes 426016 | tf_op jit(solution)/shard_map/ppermute | solution.py:18
  91.7 3.4 %convolution_convert_fusion = bf16[1664,512]{1,0:T(8,128)(2,1)} fusion(bf16[512,512]{1,0:T(8,128)(2,1)S(1)} %bitcast.29, bf16[128,1664]{1,0:T(8,128)(2,1)S(1)} %collective-permute-done.4, bf16[128,1664]{1,0:T(8,128)(2,1)} %collective-permute-done.3, bf16[128,1664]{1,0:T(8,128)(2,1)} %collective-permute-done.2, bf16[128,1664]{1,0:T(8,128)(2,1)S(1)} %bitcast.33), kind=kOutput, calls=%fused_computation.2 | convolution fusion | flops 880082944 | bytes 3932160 | tf_op jit(solution)/shard_map/dot_general | solution.py:62
  95.1 3.9 %all-to-all-done.3 = bf16[4,16,1664]{2,1,0:T(8,128)(2,1)S(1)} async-done(((bf16[4,16,1664]{2,1,0:T(8,128)(2,1)}), bf16[4,16,1664]{2,1,0:T(8,128)(2,1)S(1)}, u32[]{:S(2)}, u32[]{:S(2)}) %all-to-all-start.3) | async-done | bytes 213024 | tf_op jit(solution)/shard_map/all_to_all | solution.py:10
  99.1 0.7 multiply_convert_fusion
  (12 shorter events, 0.1 us)
Async XLA Ops:
  0.6 24.7 %copy-start = (f32[16,1664]{1,0:T(8,128)S(1)}, f32[16,1664]{1,0:T(8,128)}, u32[]{:S(2)}) copy-start(f32[16,1664]{1,0:T(8,128)} %param.9) | copy-start | bytes 319492
  2.3 26.1 %all-to-all-start = ((bf16[4,16,1664]{2,1,0:T(8,128)(2,1)}), bf16[4,16,1664]{2,1,0:T(8,128)(2,1)S(1)}, u32[]{:S(2)}, u32[]{:S(2)}) async-start(bf16[4,16,1664]{2,1,0:T(8,128)(2,1)} %broadcast_in_dim.4), calls=%async_computation | async-start | bytes 425984 | tf_op jit(solution)/shard_map/all_to_all | solution.py:10
  13.4 14.9 %collective-permute-start = (bf16[32,512]{1,0:T(8,128)(2,1)}, bf16[32,512]{1,0:T(8,128)(2,1)S(1)}, u32[]{:S(2)}, u32[]{:S(2)}) collective-permute-start(bf16[32,512]{1,0:T(8,128)(2,1)} %param.5), channel_id=1, source_target_pairs={{0,64},{64,0},{1,65},{65,1},{2,66},{66,2},{3,67},{67,3},{4,68},{68... | collective-permute-start | bytes 98312 | tf_op jit(solution)/shard_map/ppermute | solution.py:14
  25.3 3.0 %copy-start.4 = (bf16[32,512]{1,0:T(8,128)(2,1)S(1)}, bf16[32,512]{1,0:T(8,128)(2,1)}, u32[]{:S(2)}) copy-start(bf16[32,512]{1,0:T(8,128)(2,1)} %param.5) | copy-start | bytes 98308
  28.4 15.9 %copy-start.1 = (bf16[1664,512]{0,1:T(8,128)(2,1)S(1)}, bf16[1664,512]{0,1:T(8,128)(2,1)}, u32[]{:S(2)}) copy-start(bf16[1664,512]{0,1:T(8,128)(2,1)} %fusion) | copy-start | bytes 5111812
  29.3 14.9 %all-to-all-start.1 = ((bf16[8,2,32,512]{3,2,1,0:T(8,128)(2,1)}), bf16[8,2,32,512]{3,2,1,0:T(8,128)(2,1)S(1)}, u32[]{:S(2)}, u32[]{:S(2)}) async-start(bf16[8,2,32,512]{3,2,1,0:T(8,128)(2,1)} %broadcast_in_dim.5), calls=%async_computation.1 | async-start | bytes 1048576 | tf_op jit(solution)/shard_map/all_to_all | solution.py:10
  33.7 10.4 %collective-permute-start.1 = (bf16[4,16,1664]{2,1,0:T(8,128)(2,1)S(1)}, bf16[4,16,1664]{2,1,0:T(8,128)(2,1)S(1)}, u32[]{:S(2)}, u32[]{:S(2)}) collective-permute-start(bf16[4,16,1664]{2,1,0:T(8,128)(2,1)S(1)} %all-to-all-done), channel_id=1, source_target_pairs={{0,4},{4,0},{1,5},{5,1},{2,6},{6,2},{3,7},{7,3},{8,12},{12,8},{9,1... | collective-permute-start | bytes 638984 | tf_op jit(solution)/shard_map/ppermute | solution.py:14
  46.6 28.9 %all-to-all-start.2 = ((bf16[8,64,1664]{2,1,0:T(8,128)(2,1)}), bf16[8,64,1664]{2,1,0:T(8,128)(2,1)S(1)}, u32[]{:S(2)}, u32[]{:S(2)}) async-start(bf16[8,64,1664]{2,1,0:T(8,128)(2,1)} %bitcast.26), calls=%async_computation.2 | async-start | bytes 3407872 | tf_op jit(solution)/shard_map/all_to_all | solution.py:10
  53.3 32.4 %collective-permute-start.4 = (bf16[128,1664]{1,0:T(8,128)(2,1)S(1)}, bf16[128,1664]{1,0:T(8,128)(2,1)S(1)}, u32[]{:S(2)}, u32[]{:S(2)}) collective-permute-start(bf16[128,1664]{1,0:T(8,128)(2,1)S(1)} %bitcast.30), channel_id=1, source_target_pairs={{0,1},{1,2},{2,3},{3,0},{4,5},{5,6},{6,7},{7,4},{8,9},{9,10},{10,1... | collective-permute-start | bytes 1277960 | tf_op jit(solution)/shard_map/ppermute | solution.py:18
  56.7 29.0 %collective-permute-start.3 = (bf16[128,1664]{1,0:T(8,128)(2,1)S(1)}, bf16[128,1664]{1,0:T(8,128)(2,1)}, u32[]{:S(2)}, u32[]{:S(2)}) collective-permute-start(bf16[128,1664]{1,0:T(8,128)(2,1)S(1)} %bitcast.31), channel_id=1, source_target_pairs={{0,2},{1,3},{2,0},{3,1},{4,6},{5,7},{6,4},{7,5},{8,10},{9,11},{10,... | collective-permute-start | bytes 1277960 | tf_op jit(solution)/shard_map/ppermute | solution.py:18
  59.2 32.5 %collective-permute-start.2 = (bf16[128,1664]{1,0:T(8,128)(2,1)S(1)}, bf16[128,1664]{1,0:T(8,128)(2,1)}, u32[]{:S(2)}, u32[]{:S(2)}) collective-permute-start(bf16[128,1664]{1,0:T(8,128)(2,1)S(1)} %bitcast.32), channel_id=1, source_target_pairs={{0,3},{1,0},{2,1},{3,2},{4,7},{5,4},{6,5},{7,6},{8,11},{9,8},{10,9... | collective-permute-start | bytes 1277960 | tf_op jit(solution)/shard_map/ppermute | solution.py:18
  76.5 22.5 %all-to-all-start.3 = ((bf16[4,16,1664]{2,1,0:T(8,128)(2,1)}), bf16[4,16,1664]{2,1,0:T(8,128)(2,1)S(1)}, u32[]{:S(2)}, u32[]{:S(2)}) async-start(bf16[4,16,1664]{2,1,0:T(8,128)(2,1)} %bitcast.13), calls=%async_computation.3 | async-start | bytes 425984 | tf_op jit(solution)/shard_map/all_to_all | solution.py:10
  91.7 7.3 %copy-start.2 = (bf16[16,1664]{1,0:T(8,128)(2,1)S(1)}, bf16[16,1664]{1,0:T(8,128)(2,1)}, u32[]{:S(2)}) copy-start(bf16[16,1664]{1,0:T(8,128)(2,1)} %param.7) | copy-start | bytes 159748
  91.7 7.3 %copy-start.3 = (bf16[16,1664]{1,0:T(8,128)(2,1)S(1)}, bf16[16,1664]{1,0:T(8,128)(2,1)}, u32[]{:S(2)}) copy-start(bf16[16,1664]{1,0:T(8,128)(2,1)} %param.6) | copy-start | bytes 159748

commit v4 on v3

--- a/solution.py
+++ b/solution.py
@@ -32,7 +32,7 @@
     hidden = (act * up_f).astype(jnp.bfloat16)
     zb, x = lax.axis_index("zb"), lax.axis_index("x")
 
-    part = exchange(jnp.broadcast_to(hidden[None], (4,) + hidden.shape), "za")
+    part = exchange(jnp.broadcast_to(hidden[None], (4,) + hidden.shape), ("za_hi", "za_lo"))
     pair = in_order(grad_out, swap(grad_out, "zh", 2, 1), lax.axis_index("zh") == 1, 0)
     spread = (jnp.arange(width)[None] // BLOCK == jnp.arange(width // BLOCK)[:, None]).astype(jnp.float32)
     scale = lax.dot_general(weight_scales, spread, (((0,), (0,)), ((), ())), preferred_element_type=jnp.float32)
@@ -41,9 +41,9 @@
 
     mine = in_order(part, swap(part, "zb", 2, 1), zb == 1, 1).reshape(128, units)
     grads = exchange(jnp.broadcast_to(pair[None], (8,) + pair.shape), ("y", "core"))
-    grads = grads.reshape(4, 2, 2, 2, 16, width)
-    by_part = grads.transpose(1, 3, 2, 0, 4, 5).reshape(512, width)
-    by_x = grads.transpose(1, 3, 0, 2, 4, 5).reshape(4, 128, width)
+    grads = grads.reshape(2, 2, 2, 2, 2, 16, width)
+    by_part = grads.transpose(2, 4, 3, 1, 0, 5, 6).reshape(512, width)
+    by_x = grads.transpose(2, 4, 0, 1, 3, 5, 6).reshape(4, 128, width)
     partial = lax.dot_general(
         by_part, weight, (((1,), (1,)), ((), ())), preferred_element_type=jnp.float32
     ).astype(jnp.bfloat16)
@@ -54,7 +54,7 @@
     last_x = shift(mine, 1)
     far_x = shift(mine, 2)
     over_x = over_x.astype(jnp.float32).sum(0).astype(jnp.bfloat16)
-    over_z = exchange(over_x.reshape(4, 16, units), "za")
+    over_z = exchange(over_x.reshape(4, 16, units), ("za_lo", "za_hi"))
     hidden_grad = over_z.astype(jnp.float32).sum(0)
 
     all_hidden = jnp.concatenate([mine, next_x, far_x, last_x])
@@ -68,8 +68,8 @@
 
 
 def solution(mesh):
-    fine = Mesh(mesh.devices.reshape(4, 2, 2, 4, 2, 4), ("y", "zh", "core", "za", "zb", "x"))
-    row, col = ("y", "zh", "core"), ("za", "zb", "x")
+    fine = Mesh(mesh.devices.reshape(4, 2, 2, 2, 2, 2, 4), ("y", "zh", "core", "za_hi", "za_lo", "zb", "x"))
+    row, col = ("y", "zh", "core"), ("za_hi", "za_lo", "zb", "x")
     placed = (P(row, col), P(col, row), P(col, row), P(row, col), P(col, row))
     return jax.shard_map(
         per_device,

time: 100 us -> 100 us (level)
  no operation moved by 1% of the time
where the time goes in v4:
time: 100 us; the launch traced here: 99.8 us
  starting transfers between devices  55.3 us (55%)
  waiting for transfers between devices  28.7 us (29%)
  matrix products  7.61 us (8%)
  local copies, waits for them, and re-layouts  4.41 us (4%)
  other arithmetic  2.89 us (3%)
    all_to_all x4, starting transfers between devices, exchange(): return lax.all_to_all(parts, axes, split_axis=0, concat_axis=0)  31.3 us
    all_to_all x4, waiting for transfers between devices, exchange(): return lax.all_to_all(parts, axes, split_axis=0, concat_axis=0)  15.6 us
    ppermute x2, starting transfers between devices, swap(): return lax.ppermute(block, axis, [(i, i ^ stride) for i in range(size)])  13.6 us
    ppermute x3, starting transfers between devices, shift(): return lax.ppermute(block, 'x', [(i, (i + k) % 4) for i in range(4)])  10.4 us
    ppermute x2, waiting for transfers between devices, swap(): return lax.ppermute(block, axis, [(i, i ^ stride) for i in range(size)])  7.07 us
    ppermute x3, waiting for transfers between devices, shift(): return lax.ppermute(block, 'x', [(i, (i + k) % 4) for i in range(4)])  6.01 us
    dot_general x1, matrix products, per_device(): lax.dot_general(all_hidden, rolled, (((0,), (0,)), ((), ())), preferred_e...  3.43 us
    unnamed x11, local copies, waits for them, and re-layouts  2.78 us
  transfers between devices with their start and end apart: 9, of which 5 were waited for; matrix products, arithmetic and copies ran while one was open for 9% of the time, Pallas kernels for 0%

profile of v4, /device:TPU:2, one launch (start us, length us, event | category | flops | bytes accessed | tf_op | source)
XLA Modules:
  0.0 99.8 jit_solution(13613859190038238327)
XLA Ops:
  0.6 0.0 copy-start
  0.6 0.9 fusion.9
  1.6 0.7 broadcast_in_dim.4
  2.3 11.2 %all-to-all-start = ((bf16[4,16,1664]{2,1,0:T(8,128)(2,1)}), bf16[4,16,1664]{2,1,0:T(8,128)(2,1)S(1)}, u32[]{:S(2)}, u32[]{:S(2)}) async-start(bf16[4,16,1664]{2,1,0:T(8,128)(2,1)} %broadcast_in_dim.4), calls=%async_computation | async-start | bytes 425984 | tf_op jit(solution)/shard_map/all_to_all | solution.py:10
  13.4 9.1 %collective-permute-start = (bf16[32,512]{1,0:T(8,128)(2,1)}, bf16[32,512]{1,0:T(8,128)(2,1)S(1)}, u32[]{:S(2)}, u32[]{:S(2)}) collective-permute-start(bf16[32,512]{1,0:T(8,128)(2,1)} %param.5), channel_id=1, source_target_pairs={{0,64},{64,0},{1,65},{65,1},{2,66},{66,2},{3,67},{67,3},{4,68},{68... | collective-permute-start | bytes 98312 | tf_op jit(solution)/shard_map/ppermute | solution.py:14
  22.6 2.8 %copy.14 = bf16[1664,512]{0,1:T(8,128)(2,1)S(1)} copy(bf16[1664,512]{1,0:T(8,128)(2,1)} %param.8) | data formatting | bytes 3407872 | tf_op args[3]
  25.3 0.0 copy-start.4
  25.3 1.9 %fusion = bf16[1664,512]{0,1:T(8,128)(2,1)} fusion(bf16[1664,512]{0,1:T(8,128)(2,1)S(1)} %copy.14, f32[16,1664]{1,0:T(8,128)S(1)} %copy-done, s32[512]{0:T(512)S(1)} %add_select_fusion), kind=kOutput, calls=%fused_computation.1 | convolution fusion | flops 29827072 | bytes 3516416 | tf_op jit(solution)/shard_map/dot_general | solution.py:38
  27.2 1.2 %collective-permute-done = bf16[32,512]{1,0:T(8,128)(2,1)S(1)} collective-permute-done((bf16[32,512]{1,0:T(8,128)(2,1)}, bf16[32,512]{1,0:T(8,128)(2,1)S(1)}, u32[]{:S(2)}, u32[]{:S(2)}) %collective-permute-start) | collective-permute-done | bytes 32800 | tf_op jit(solution)/shard_map/ppermute | solution.py:14
  28.4 0.0 copy-start.1
  28.4 0.0 all-to-all-done
  28.4 0.8 broadcast_in_dim.5
  29.3 4.5 %all-to-all-start.1 = ((bf16[8,2,32,512]{3,2,1,0:T(8,128)(2,1)}), bf16[8,2,32,512]{3,2,1,0:T(8,128)(2,1)S(1)}, u32[]{:S(2)}, u32[]{:S(2)}) async-start(bf16[8,2,32,512]{3,2,1,0:T(8,128)(2,1)} %broadcast_in_dim.5), calls=%async_computation.1 | async-start | bytes 1048576 | tf_op jit(solution)/shard_map/all_to_all | solution.py:10
  33.7 4.5 %collective-permute-start.1 = (bf16[4,16,1664]{2,1,0:T(8,128)(2,1)S(1)}, bf16[4,16,1664]{2,1,0:T(8,128)(2,1)S(1)}, u32[]{:S(2)}, u32[]{:S(2)}) collective-permute-start(bf16[4,16,1664]{2,1,0:T(8,128)(2,1)S(1)} %all-to-all-done), channel_id=1, source_target_pairs={{0,4},{4,0},{1,5},{5,1},{2,6},{6,2},{3,7},{7,3},{8,12},{12,8},{9,1... | collective-permute-start | bytes 638984 | tf_op jit(solution)/shard_map/ppermute | solution.py:14
  38.2 5.9 %collective-permute-done.1 = bf16[4,16,1664]{2,1,0:T(8,128)(2,1)S(1)} collective-permute-done((bf16[4,16,1664]{2,1,0:T(8,128)(2,1)S(1)}, bf16[4,16,1664]{2,1,0:T(8,128)(2,1)S(1)}, u32[]{:S(2)}, u32[]{:S(2)}) %collective-permute-start.1) | collective-permute-done | bytes 213024 | tf_op jit(solution)/shard_map/ppermute | solution.py:14
  44.1 0.1 maximum_select_fusion
  44.2 0.0 all-to-all-done.1
  44.3 2.3 %convolution_convert_fusion.1 = bf16[512,1664]{1,0:T(8,128)(2,1)} fusion(bf16[512,512]{1,0:T(8,128)(2,1)S(1)} %bitcast.28, bf16[1664,512]{0,1:T(8,128)(2,1)S(1)} %copy-done.1), kind=kOutput, calls=%fused_computation.3 | convolution fusion | flops 873267200 | bytes 3932160 | tf_op jit(solution)/shard_map/dot_general | solution.py:47
  46.6 6.7 %all-to-all-start.2 = ((bf16[8,64,1664]{2,1,0:T(8,128)(2,1)}), bf16[8,64,1664]{2,1,0:T(8,128)(2,1)S(1)}, u32[]{:S(2)}, u32[]{:S(2)}) async-start(bf16[8,64,1664]{2,1,0:T(8,128)(2,1)} %bitcast.26), calls=%async_computation.2 | async-start | bytes 3407872 | tf_op jit(solution)/shard_map/all_to_all | solution.py:10
  53.3 3.4 %collective-permute-start.4 = (bf16[128,1664]{1,0:T(8,128)(2,1)S(1)}, bf16[128,1664]{1,0:T(8,128)(2,1)S(1)}, u32[]{:S(2)}, u32[]{:S(2)}) collective-permute-start(bf16[128,1664]{1,0:T(8,128)(2,1)S(1)} %bitcast.30), channel_id=1, source_target_pairs={{0,1},{1,2},{2,3},{3,0},{4,5},{5,6},{6,7},{7,4},{8,9},{9,10},{10,1... | collective-permute-start | bytes 1277960 | tf_op jit(solution)/shard_map/ppermute | solution.py:18
  56.7 2.5 %collective-permute-start.3 = (bf16[128,1664]{1,0:T(8,128)(2,1)S(1)}, bf16[128,1664]{1,0:T(8,128)(2,1)}, u32[]{:S(2)}, u32[]{:S(2)}) collective-permute-start(bf16[128,1664]{1,0:T(8,128)(2,1)S(1)} %bitcast.31), channel_id=1, source_target_pairs={{0,2},{1,3},{2,0},{3,1},{4,6},{5,7},{6,4},{7,5},{8,10},{9,11},{10,... | collective-permute-start | bytes 1277960 | tf_op jit(solution)/shard_map/ppermute | solution.py:18
  59.2 4.5 %collective-permute-start.2 = (bf16[128,1664]{1,0:T(8,128)(2,1)S(1)}, bf16[128,1664]{1,0:T(8,128)(2,1)}, u32[]{:S(2)}, u32[]{:S(2)}) collective-permute-start(bf16[128,1664]{1,0:T(8,128)(2,1)S(1)} %bitcast.32), channel_id=1, source_target_pairs={{0,3},{1,0},{2,1},{3,2},{4,7},{5,4},{6,5},{7,6},{8,11},{9,8},{10,9... | collective-permute-start | bytes 1277960 | tf_op jit(solution)/shard_map/ppermute | solution.py:18
  63.8 11.7 %all-to-all-done.2 = bf16[8,64,1664]{2,1,0:T(8,128)(2,1)S(1)} async-done(((bf16[8,64,1664]{2,1,0:T(8,128)(2,1)}), bf16[8,64,1664]{2,1,0:T(8,128)(2,1)S(1)}, u32[]{:S(2)}, u32[]{:S(2)}) %all-to-all-start.2) | async-done | bytes 1703968 | tf_op jit(solution)/shard_map/all_to_all | solution.py:10
  75.5 1.0 reduce_sum.21
  76.5 8.9 %all-to-all-start.3 = ((bf16[4,16,1664]{2,1,0:T(8,128)(2,1)}), bf16[4,16,1664]{2,1,0:T(8,128)(2,1)S(1)}, u32[]{:S(2)}, u32[]{:S(2)}) async-start(bf16[4,16,1664]{2,1,0:T(8,128)(2,1)} %bitcast.13), calls=%async_computation.3 | async-start | bytes 425984 | tf_op jit(solution)/shard_map/all_to_all | solution.py:10
  85.5 0.2 fusion.8
  85.7 0.0 collective-permute-done.4
  85.7 0.0 collective-permute-done.3
  85.7 6.0 %collective-permute-done.2 = bf16[128,1664]{1,0:T(8,128)(2,1)} collective-permute-done((bf16[128,1664]{1,0:T(8,128)(2,1)S(1)}, bf16[128,1664]{1,0:T(8,128)(2,1)}, u32[]{:S(2)}, u32[]{:S(2)}) %collective-permute-start.2) | collective-permute-done | bytes 426016 | tf_op jit(solution)/shard_map/ppermute | solution.py:18
  91.7 3.4 %convolution_convert_fusion = bf16[1664,512]{1,0:T(8,128)(2,1)} fusion(bf16[512,512]{1,0:T(8,128)(2,1)S(1)} %bitcast.29, bf16[128,1664]{1,0:T(8,128)(2,1)S(1)} %collective-permute-done.4, bf16[128,1664]{1,0:T(8,128)(2,1)} %collective-permute-done.3, bf16[128,1664]{1,0:T(8,128)(2,1)} %collective-permute-done.2, bf16[128,1664]{1,0:T(8,128)(2,1)S(1)} %bitcast.33), kind=kOutput, calls=%fused_computation.2 | convolution fusion | flops 880082944 | bytes 3932160 | tf_op jit(solution)/shard_map/dot_general | solution.py:62
  95.1 3.9 %all-to-all-done.3 = bf16[4,16,1664]{2,1,0:T(8,128)(2,1)S(1)} async-done(((bf16[4,16,1664]{2,1,0:T(8,128)(2,1)}), bf16[4,16,1664]{2,1,0:T(8,128)(2,1)S(1)}, u32[]{:S(2)}, u32[]{:S(2)}) %all-to-all-start.3) | async-done | bytes 213024 | tf_op jit(solution)/shard_map/all_to_all | solution.py:10
  99.1 0.7 multiply_convert_fusion
  (12 shorter events, 0.1 us)
Async XLA Ops:
  0.6 24.7 %copy-start = (f32[16,1664]{1,0:T(8,128)S(1)}, f32[16,1664]{1,0:T(8,128)}, u32[]{:S(2)}) copy-start(f32[16,1664]{1,0:T(8,128)} %param.9) | copy-start | bytes 319492
  2.3 26.1 %all-to-all-start = ((bf16[4,16,1664]{2,1,0:T(8,128)(2,1)}), bf16[4,16,1664]{2,1,0:T(8,128)(2,1)S(1)}, u32[]{:S(2)}, u32[]{:S(2)}) async-start(bf16[4,16,1664]{2,1,0:T(8,128)(2,1)} %broadcast_in_dim.4), calls=%async_computation | async-start | bytes 425984 | tf_op jit(solution)/shard_map/all_to_all | solution.py:10
  13.4 14.9 %collective-permute-start = (bf16[32,512]{1,0:T(8,128)(2,1)}, bf16[32,512]{1,0:T(8,128)(2,1)S(1)}, u32[]{:S(2)}, u32[]{:S(2)}) collective-permute-start(bf16[32,512]{1,0:T(8,128)(2,1)} %param.5), channel_id=1, source_target_pairs={{0,64},{64,0},{1,65},{65,1},{2,66},{66,2},{3,67},{67,3},{4,68},{68... | collective-permute-start | bytes 98312 | tf_op jit(solution)/shard_map/ppermute | solution.py:14
  25.3 3.0 %copy-start.4 = (bf16[32,512]{1,0:T(8,128)(2,1)S(1)}, bf16[32,512]{1,0:T(8,128)(2,1)}, u32[]{:S(2)}) copy-start(bf16[32,512]{1,0:T(8,128)(2,1)} %param.5) | copy-start | bytes 98308
  28.4 15.9 %copy-start.1 = (bf16[1664,512]{0,1:T(8,128)(2,1)S(1)}, bf16[1664,512]{0,1:T(8,128)(2,1)}, u32[]{:S(2)}) copy-start(bf16[1664,512]{0,1:T(8,128)(2,1)} %fusion) | copy-start | bytes 5111812
  29.3 14.9 %all-to-all-start.1 = ((bf16[8,2,32,512]{3,2,1,0:T(8,128)(2,1)}), bf16[8,2,32,512]{3,2,1,0:T(8,128)(2,1)S(1)}, u32[]{:S(2)}, u32[]{:S(2)}) async-start(bf16[8,2,32,512]{3,2,1,0:T(8,128)(2,1)} %broadcast_in_dim.5), calls=%async_computation.1 | async-start | bytes 1048576 | tf_op jit(solution)/shard_map/all_to_all | solution.py:10
  33.7 10.4 %collective-permute-start.1 = (bf16[4,16,1664]{2,1,0:T(8,128)(2,1)S(1)}, bf16[4,16,1664]{2,1,0:T(8,128)(2,1)S(1)}, u32[]{:S(2)}, u32[]{:S(2)}) collective-permute-start(bf16[4,16,1664]{2,1,0:T(8,128)(2,1)S(1)} %all-to-all-done), channel_id=1, source_target_pairs={{0,4},{4,0},{1,5},{5,1},{2,6},{6,2},{3,7},{7,3},{8,12},{12,8},{9,1... | collective-permute-start | bytes 638984 | tf_op jit(solution)/shard_map/ppermute | solution.py:14
  46.6 28.9 %all-to-all-start.2 = ((bf16[8,64,1664]{2,1,0:T(8,128)(2,1)}), bf16[8,64,1664]{2,1,0:T(8,128)(2,1)S(1)}, u32[]{:S(2)}, u32[]{:S(2)}) async-start(bf16[8,64,1664]{2,1,0:T(8,128)(2,1)} %bitcast.26), calls=%async_computation.2 | async-start | bytes 3407872 | tf_op jit(solution)/shard_map/all_to_all | solution.py:10
  53.3 32.4 %collective-permute-start.4 = (bf16[128,1664]{1,0:T(8,128)(2,1)S(1)}, bf16[128,1664]{1,0:T(8,128)(2,1)S(1)}, u32[]{:S(2)}, u32[]{:S(2)}) collective-permute-start(bf16[128,1664]{1,0:T(8,128)(2,1)S(1)} %bitcast.30), channel_id=1, source_target_pairs={{0,1},{1,2},{2,3},{3,0},{4,5},{5,6},{6,7},{7,4},{8,9},{9,10},{10,1... | collective-permute-start | bytes 1277960 | tf_op jit(solution)/shard_map/ppermute | solution.py:18
  56.7 29.0 %collective-permute-start.3 = (bf16[128,1664]{1,0:T(8,128)(2,1)S(1)}, bf16[128,1664]{1,0:T(8,128)(2,1)}, u32[]{:S(2)}, u32[]{:S(2)}) collective-permute-start(bf16[128,1664]{1,0:T(8,128)(2,1)S(1)} %bitcast.31), channel_id=1, source_target_pairs={{0,2},{1,3},{2,0},{3,1},{4,6},{5,7},{6,4},{7,5},{8,10},{9,11},{10,... | collective-permute-start | bytes 1277960 | tf_op jit(solution)/shard_map/ppermute | solution.py:18
  59.2 32.5 %collective-permute-start.2 = (bf16[128,1664]{1,0:T(8,128)(2,1)S(1)}, bf16[128,1664]{1,0:T(8,128)(2,1)}, u32[]{:S(2)}, u32[]{:S(2)}) collective-permute-start(bf16[128,1664]{1,0:T(8,128)(2,1)S(1)} %bitcast.32), channel_id=1, source_target_pairs={{0,3},{1,0},{2,1},{3,2},{4,7},{5,4},{6,5},{7,6},{8,11},{9,8},{10,9... | collective-permute-start | bytes 1277960 | tf_op jit(solution)/shard_map/ppermute | solution.py:18
  76.5 22.5 %all-to-all-start.3 = ((bf16[4,16,1664]{2,1,0:T(8,128)(2,1)}), bf16[4,16,1664]{2,1,0:T(8,128)(2,1)S(1)}, u32[]{:S(2)}, u32[]{:S(2)}) async-start(bf16[4,16,1664]{2,1,0:T(8,128)(2,1)} %bitcast.13), calls=%async_computation.3 | async-start | bytes 425984 | tf_op jit(solution)/shard_map/all_to_all | solution.py:10
  91.7 7.3 %copy-start.2 = (bf16[16,1664]{1,0:T(8,128)(2,1)S(1)}, bf16[16,1664]{1,0:T(8,128)(2,1)}, u32[]{:S(2)}) copy-start(bf16[16,1664]{1,0:T(8,128)(2,1)} %param.7) | copy-start | bytes 159748
  91.7 7.3 %copy-start.3 = (bf16[16,1664]{1,0:T(8,128)(2,1)S(1)}, bf16[16,1664]{1,0:T(8,128)(2,1)}, u32[]{:S(2)}) copy-start(bf16[16,1664]{1,0:T(8,128)(2,1)} %param.6) | copy-start | bytes 159748

commit v5 on v4

--- a/solution.py
+++ b/solution.py
@@ -57,8 +57,9 @@
     over_z = exchange(over_x.reshape(4, 16, units), ("za_lo", "za_hi"))
     hidden_grad = over_z.astype(jnp.float32).sum(0)
 
-    all_hidden = jnp.concatenate([mine, next_x, far_x, last_x])
-    rolled = lax.dynamic_slice_in_dim(jnp.concatenate([by_x, by_x]), x, 4).reshape(512, width)
+    all_hidden = jnp.concatenate([mine, far_x, next_x, last_x])
+    twice = jnp.concatenate([by_x, by_x])
+    rolled = jnp.concatenate([lax.dynamic_slice_in_dim(twice, x + k, 1) for k in (0, 2, 1, 3)]).reshape(512, width)
     weight_grad = lax.dot_general(
         all_hidden, rolled, (((0,), (0,)), ((), ())), preferred_element_type=jnp.float32
     ).astype(jnp.bfloat16)

time: 100 us -> 100 us (level)
  no operation moved by 1% of the time
where the time goes in v5:
time: 100 us; the launch traced here: 99.7 us
  starting transfers between devices  54.7 us (55%)
  waiting for transfers between devices  29.2 us (29%)
  matrix products  7.61 us (8%)
  local copies, waits for them, and re-layouts  4.4 us (4%)
  other arithmetic  2.96 us (3%)
    all_to_all x4, starting transfers between devices, exchange(): return lax.all_to_all(parts, axes, split_axis=0, concat_axis=0)  31.3 us
    all_to_all x4, waiting for transfers between devices, exchange(): return lax.all_to_all(parts, axes, split_axis=0, concat_axis=0)  15.7 us
    ppermute x2, starting transfers between devices, swap(): return lax.ppermute(block, axis, [(i, i ^ stride) for i in range(size)])  13.6 us
    ppermute x3, starting transfers between devices, shift(): return lax.ppermute(block, 'x', [(i, (i + k) % 4) for i in range(4)])  9.81 us
    ppermute x2, waiting for transfers between devices, swap(): return lax.ppermute(block, axis, [(i, i ^ stride) for i in range(size)])  7.07 us
    ppermute x3, waiting for transfers between devices, shift(): return lax.ppermute(block, 'x', [(i, (i + k) % 4) for i in range(4)])  6.42 us
    dot_general x1, matrix products, per_device(): lax.dot_general(all_hidden, rolled, (((0,), (0,)), ((), ())), preferred_e...  3.43 us
    unnamed x11, local copies, waits for them, and re-layouts  2.78 us
  transfers between devices with their start and end apart: 9, of which 5 were waited for; matrix products, arithmetic and copies ran while one was open for 9% of the time, Pallas kernels for 0%

profile of v5, /device:TPU:2, one launch (start us, length us, event | category | flops | bytes accessed | tf_op | source)
XLA Modules:
  0.0 99.7 jit_solution(5631216019247802107)
XLA Ops:
  0.6 0.0 copy-start
  0.6 0.9 fusion.12
  1.6 0.7 broadcast_in_dim.4
  2.3 11.2 %all-to-all-start = ((bf16[4,16,1664]{2,1,0:T(8,128)(2,1)}), bf16[4,16,1664]{2,1,0:T(8,128)(2,1)S(1)}, u32[]{:S(2)}, u32[]{:S(2)}) async-start(bf16[4,16,1664]{2,1,0:T(8,128)(2,1)} %broadcast_in_dim.4), calls=%async_computation | async-start | bytes 425984 | tf_op jit(solution)/shard_map/all_to_all | solution.py:10
  13.4 9.1 %collective-permute-start = (bf16[32,512]{1,0:T(8,128)(2,1)}, bf16[32,512]{1,0:T(8,128)(2,1)S(1)}, u32[]{:S(2)}, u32[]{:S(2)}) collective-permute-start(bf16[32,512]{1,0:T(8,128)(2,1)} %param.5), channel_id=1, source_target_pairs={{0,64},{64,0},{1,65},{65,1},{2,66},{66,2},{3,67},{67,3},{4,68},{68... | collective-permute-start | bytes 98312 | tf_op jit(solution)/shard_map/ppermute | solution.py:14
  22.5 2.8 %copy.14 = bf16[1664,512]{0,1:T(8,128)(2,1)S(1)} copy(bf16[1664,512]{1,0:T(8,128)(2,1)} %param.8) | data formatting | bytes 3407872 | tf_op args[3]
  25.3 0.0 copy-start.4
  25.3 1.9 %fusion = bf16[1664,512]{0,1:T(8,128)(2,1)} fusion(bf16[1664,512]{0,1:T(8,128)(2,1)S(1)} %copy.14, f32[16,1664]{1,0:T(8,128)S(1)} %copy-done, s32[512]{0:T(512)S(1)} %add_select_fusion), kind=kOutput, calls=%fused_computation.1 | convolution fusion | flops 29827072 | bytes 3516416 | tf_op jit(solution)/shard_map/dot_general | solution.py:38
  27.2 1.2 %collective-permute-done = bf16[32,512]{1,0:T(8,128)(2,1)S(1)} collective-permute-done((bf16[32,512]{1,0:T(8,128)(2,1)}, bf16[32,512]{1,0:T(8,128)(2,1)S(1)}, u32[]{:S(2)}, u32[]{:S(2)}) %collective-permute-start) | collective-permute-done | bytes 32800 | tf_op jit(solution)/shard_map/ppermute | solution.py:14
  28.4 0.0 copy-start.1
  28.4 0.0 all-to-all-done
  28.4 0.8 broadcast_in_dim.5
  29.2 4.5 %all-to-all-start.1 = ((bf16[8,2,32,512]{3,2,1,0:T(8,128)(2,1)}), bf16[8,2,32,512]{3,2,1,0:T(8,128)(2,1)S(1)}, u32[]{:S(2)}, u32[]{:S(2)}) async-start(bf16[8,2,32,512]{3,2,1,0:T(8,128)(2,1)} %broadcast_in_dim.5), calls=%async_computation.1 | async-start | bytes 1048576 | tf_op jit(solution)/shard_map/all_to_all | solution.py:10
  33.7 4.5 %collective-permute-start.1 = (bf16[4,16,1664]{2,1,0:T(8,128)(2,1)S(1)}, bf16[4,16,1664]{2,1,0:T(8,128)(2,1)S(1)}, u32[]{:S(2)}, u32[]{:S(2)}) collective-permute-start(bf16[4,16,1664]{2,1,0:T(8,128)(2,1)S(1)} %all-to-all-done), channel_id=1, source_target_pairs={{0,4},{4,0},{1,5},{5,1},{2,6},{6,2},{3,7},{7,3},{8,12},{12,8},{9,1... | collective-permute-start | bytes 638984 | tf_op jit(solution)/shard_map/ppermute | solution.py:14
  38.2 5.9 %collective-permute-done.1 = bf16[4,16,1664]{2,1,0:T(8,128)(2,1)S(1)} collective-permute-done((bf16[4,16,1664]{2,1,0:T(8,128)(2,1)S(1)}, bf16[4,16,1664]{2,1,0:T(8,128)(2,1)S(1)}, u32[]{:S(2)}, u32[]{:S(2)}) %collective-permute-start.1) | collective-permute-done | bytes 213024 | tf_op jit(solution)/shard_map/ppermute | solution.py:14
  44.1 0.1 maximum_select_fusion
  44.2 0.0 all-to-all-done.1
  44.2 2.3 %convolution_convert_fusion.1 = bf16[512,1664]{1,0:T(8,128)(2,1)} fusion(bf16[512,512]{1,0:T(8,128)(2,1)S(1)} %bitcast.29, bf16[1664,512]{0,1:T(8,128)(2,1)S(1)} %copy-done.1), kind=kOutput, calls=%fused_computation.3 | convolution fusion | flops 873267200 | bytes 3932160 | tf_op jit(solution)/shard_map/dot_general | solution.py:47
  46.6 6.7 %all-to-all-start.2 = ((bf16[8,64,1664]{2,1,0:T(8,128)(2,1)}), bf16[8,64,1664]{2,1,0:T(8,128)(2,1)S(1)}, u32[]{:S(2)}, u32[]{:S(2)}) async-start(bf16[8,64,1664]{2,1,0:T(8,128)(2,1)} %bitcast.26), calls=%async_computation.2 | async-start | bytes 3407872 | tf_op jit(solution)/shard_map/all_to_all | solution.py:10
  53.3 3.4 %collective-permute-start.4 = (bf16[128,1664]{1,0:T(8,128)(2,1)S(1)}, bf16[128,1664]{1,0:T(8,128)(2,1)S(1)}, u32[]{:S(2)}, u32[]{:S(2)}) collective-permute-start(bf16[128,1664]{1,0:T(8,128)(2,1)S(1)} %bitcast.30), channel_id=1, source_target_pairs={{0,1},{1,2},{2,3},{3,0},{4,5},{5,6},{6,7},{7,4},{8,9},{9,10},{10,1... | collective-permute-start | bytes 1277960 | tf_op jit(solution)/shard_map/ppermute | solution.py:18
  56.7 2.5 %collective-permute-start.3 = (bf16[128,1664]{1,0:T(8,128)(2,1)S(1)}, bf16[128,1664]{1,0:T(8,128)(2,1)}, u32[]{:S(2)}, u32[]{:S(2)}) collective-permute-start(bf16[128,1664]{1,0:T(8,128)(2,1)S(1)} %bitcast.31), channel_id=1, source_target_pairs={{0,3},{1,0},{2,1},{3,2},{4,7},{5,4},{6,5},{7,6},{8,11},{9,8},{10,9... | collective-permute-start | bytes 1277960 | tf_op jit(solution)/shard_map/ppermute | solution.py:18
  59.1 4.0 %collective-permute-start.2 = (bf16[128,1664]{1,0:T(8,128)(2,1)S(1)}, bf16[128,1664]{1,0:T(8,128)(2,1)}, u32[]{:S(2)}, u32[]{:S(2)}) collective-permute-start(bf16[128,1664]{1,0:T(8,128)(2,1)S(1)} %bitcast.32), channel_id=1, source_target_pairs={{0,2},{1,3},{2,0},{3,1},{4,6},{5,7},{6,4},{7,5},{8,10},{9,11},{10,... | collective-permute-start | bytes 1277960 | tf_op jit(solution)/shard_map/ppermute | solution.py:18
  63.1 12.3 %all-to-all-done.2 = bf16[8,64,1664]{2,1,0:T(8,128)(2,1)S(1)} async-done(((bf16[8,64,1664]{2,1,0:T(8,128)(2,1)}), bf16[8,64,1664]{2,1,0:T(8,128)(2,1)S(1)}, u32[]{:S(2)}, u32[]{:S(2)}) %all-to-all-start.2) | async-done | bytes 1703968 | tf_op jit(solution)/shard_map/all_to_all | solution.py:10
  75.4 1.0 reduce_sum.21
  76.4 8.9 %all-to-all-start.3 = ((bf16[4,16,1664]{2,1,0:T(8,128)(2,1)}), bf16[4,16,1664]{2,1,0:T(8,128)(2,1)S(1)}, u32[]{:S(2)}, u32[]{:S(2)}) async-start(bf16[4,16,1664]{2,1,0:T(8,128)(2,1)} %bitcast.13), calls=%async_computation.3 | async-start | bytes 425984 | tf_op jit(solution)/shard_map/all_to_all | solution.py:10
  85.4 0.2 fusion.9
  85.6 0.1 pad_maximum_fusion
  85.7 0.0 collective-permute-done.3
  85.7 6.4 %collective-permute-done.2 = bf16[128,1664]{1,0:T(8,128)(2,1)} collective-permute-done((bf16[128,1664]{1,0:T(8,128)(2,1)S(1)}, bf16[128,1664]{1,0:T(8,128)(2,1)}, u32[]{:S(2)}, u32[]{:S(2)}) %collective-permute-start.2) | collective-permute-done | bytes 426016 | tf_op jit(solution)/shard_map/ppermute | solution.py:18
  92.1 3.4 %convolution_convert_fusion = bf16[1664,512]{1,0:T(8,128)(2,1)} fusion(bf16[512,512]{1,0:T(8,128)(2,1)S(1)} %bitcast.28, bf16[128,1664]{1,0:T(8,128)(2,1)S(1)} %collective-permute-done.4, bf16[128,1664]{1,0:T(8,128)(2,1)} %collective-permute-done.3, bf16[128,1664]{1,0:T(8,128)(2,1)} %collective-permute-done.2, bf16[128,1664]{1,0:T(8,128)(2,1)S(1)} %bitcast.33), kind=kOutput, calls=%fused_computation.2 | convolution fusion | flops 880082944 | bytes 3932160 | tf_op jit(solution)/shard_map/dot_general | solution.py:63
  95.6 3.4 %all-to-all-done.3 = bf16[4,16,1664]{2,1,0:T(8,128)(2,1)S(1)} async-done(((bf16[4,16,1664]{2,1,0:T(8,128)(2,1)}), bf16[4,16,1664]{2,1,0:T(8,128)(2,1)S(1)}, u32[]{:S(2)}, u32[]{:S(2)}) %all-to-all-start.3) | async-done | bytes 213024 | tf_op jit(solution)/shard_map/all_to_all | solution.py:10
  99.0 0.7 multiply_convert_fusion
  (13 shorter events, 0.1 us)
Async XLA Ops:
  0.6 24.7 %copy-start = (f32[16,1664]{1,0:T(8,128)S(1)}, f32[16,1664]{1,0:T(8,128)}, u32[]{:S(2)}) copy-start(f32[16,1664]{1,0:T(8,128)} %param.9) | copy-start | bytes 319492
  2.3 26.1 %all-to-all-start = ((bf16[4,16,1664]{2,1,0:T(8,128)(2,1)}), bf16[4,16,1664]{2,1,0:T(8,128)(2,1)S(1)}, u32[]{:S(2)}, u32[]{:S(2)}) async-start(bf16[4,16,1664]{2,1,0:T(8,128)(2,1)} %broadcast_in_dim.4), calls=%async_computation | async-start | bytes 425984 | tf_op jit(solution)/shard_map/all_to_all | solution.py:10
  13.4 14.9 %collective-permute-start = (bf16[32,512]{1,0:T(8,128)(2,1)}, bf16[32,512]{1,0:T(8,128)(2,1)S(1)}, u32[]{:S(2)}, u32[]{:S(2)}) collective-permute-start(bf16[32,512]{1,0:T(8,128)(2,1)} %param.5), channel_id=1, source_target_pairs={{0,64},{64,0},{1,65},{65,1},{2,66},{66,2},{3,67},{67,3},{4,68},{68... | collective-permute-start | bytes 98312 | tf_op jit(solution)/shard_map/ppermute | solution.py:14
  25.3 3.0 %copy-start.4 = (bf16[32,512]{1,0:T(8,128)(2,1)S(1)}, bf16[32,512]{1,0:T(8,128)(2,1)}, u32[]{:S(2)}) copy-start(bf16[32,512]{1,0:T(8,128)(2,1)} %param.5) | copy-start | bytes 98308
  28.4 15.9 %copy-start.1 = (bf16[1664,512]{0,1:T(8,128)(2,1)S(1)}, bf16[1664,512]{0,1:T(8,128)(2,1)}, u32[]{:S(2)}) copy-start(bf16[1664,512]{0,1:T(8,128)(2,1)} %fusion) | copy-start | bytes 5111812
  29.2 14.9 %all-to-all-start.1 = ((bf16[8,2,32,512]{3,2,1,0:T(8,128)(2,1)}), bf16[8,2,32,512]{3,2,1,0:T(8,128)(2,1)S(1)}, u32[]{:S(2)}, u32[]{:S(2)}) async-start(bf16[8,2,32,512]{3,2,1,0:T(8,128)(2,1)} %broadcast_in_dim.5), calls=%async_computation.1 | async-start | bytes 1048576 | tf_op jit(solution)/shard_map/all_to_all | solution.py:10
  33.7 10.4 %collective-permute-start.1 = (bf16[4,16,1664]{2,1,0:T(8,128)(2,1)S(1)}, bf16[4,16,1664]{2,1,0:T(8,128)(2,1)S(1)}, u32[]{:S(2)}, u32[]{:S(2)}) collective-permute-start(bf16[4,16,1664]{2,1,0:T(8,128)(2,1)S(1)} %all-to-all-done), channel_id=1, source_target_pairs={{0,4},{4,0},{1,5},{5,1},{2,6},{6,2},{3,7},{7,3},{8,12},{12,8},{9,1... | collective-permute-start | bytes 638984 | tf_op jit(solution)/shard_map/ppermute | solution.py:14
  46.6 28.9 %all-to-all-start.2 = ((bf16[8,64,1664]{2,1,0:T(8,128)(2,1)}), bf16[8,64,1664]{2,1,0:T(8,128)(2,1)S(1)}, u32[]{:S(2)}, u32[]{:S(2)}) async-start(bf16[8,64,1664]{2,1,0:T(8,128)(2,1)} %bitcast.26), calls=%async_computation.2 | async-start | bytes 3407872 | tf_op jit(solution)/shard_map/all_to_all | solution.py:10
  53.3 32.4 %collective-permute-start.4 = (bf16[128,1664]{1,0:T(8,128)(2,1)S(1)}, bf16[128,1664]{1,0:T(8,128)(2,1)S(1)}, u32[]{:S(2)}, u32[]{:S(2)}) collective-permute-start(bf16[128,1664]{1,0:T(8,128)(2,1)S(1)} %bitcast.30), channel_id=1, source_target_pairs={{0,1},{1,2},{2,3},{3,0},{4,5},{5,6},{6,7},{7,4},{8,9},{9,10},{10,1... | collective-permute-start | bytes 1277960 | tf_op jit(solution)/shard_map/ppermute | solution.py:18
  56.7 29.0 %collective-permute-start.3 = (bf16[128,1664]{1,0:T(8,128)(2,1)S(1)}, bf16[128,1664]{1,0:T(8,128)(2,1)}, u32[]{:S(2)}, u32[]{:S(2)}) collective-permute-start(bf16[128,1664]{1,0:T(8,128)(2,1)S(1)} %bitcast.31), channel_id=1, source_target_pairs={{0,3},{1,0},{2,1},{3,2},{4,7},{5,4},{6,5},{7,6},{8,11},{9,8},{10,9... | collective-permute-start | bytes 1277960 | tf_op jit(solution)/shard_map/ppermute | solution.py:18
  59.1 33.0 %collective-permute-start.2 = (bf16[128,1664]{1,0:T(8,128)(2,1)S(1)}, bf16[128,1664]{1,0:T(8,128)(2,1)}, u32[]{:S(2)}, u32[]{:S(2)}) collective-permute-start(bf16[128,1664]{1,0:T(8,128)(2,1)S(1)} %bitcast.32), channel_id=1, source_target_pairs={{0,2},{1,3},{2,0},{3,1},{4,6},{5,7},{6,4},{7,5},{8,10},{9,11},{10,... | collective-permute-start | bytes 1277960 | tf_op jit(solution)/shard_map/ppermute | solution.py:18
  76.4 22.6 %all-to-all-start.3 = ((bf16[4,16,1664]{2,1,0:T(8,128)(2,1)}), bf16[4,16,1664]{2,1,0:T(8,128)(2,1)S(1)}, u32[]{:S(2)}, u32[]{:S(2)}) async-start(bf16[4,16,1664]{2,1,0:T(8,128)(2,1)} %bitcast.13), calls=%async_computation.3 | async-start | bytes 425984 | tf_op jit(solution)/shard_map/all_to_all | solution.py:10
  92.1 6.9 %copy-start.2 = (bf16[16,1664]{1,0:T(8,128)(2,1)S(1)}, bf16[16,1664]{1,0:T(8,128)(2,1)}, u32[]{:S(2)}) copy-start(bf16[16,1664]{1,0:T(8,128)(2,1)} %param.7) | copy-start | bytes 159748
  92.1 6.9 %copy-start.3 = (bf16[16,1664]{1,0:T(8,128)(2,1)S(1)}, bf16[16,1664]{1,0:T(8,128)(2,1)}, u32[]{:S(2)}) copy-start(bf16[16,1664]{1,0:T(8,128)(2,1)} %param.6) | copy-start | bytes 159748

commit v6 on v3

--- a/solution.py
+++ b/solution.py
@@ -12,10 +12,6 @@
 
 def swap(block, axis, size, stride):
     return lax.ppermute(block, axis, [(i, i ^ stride) for i in range(size)])
-
-
-def shift(block, k):
-    return lax.ppermute(block, "x", [(i, (i + k) % 4) for i in range(4)])
 
 
 def in_order(mine, other, upper, axis):
@@ -50,15 +46,13 @@
     partial, mine = lax.optimization_barrier((partial, mine))
 
     over_x = exchange(partial.reshape(8, 64, units), ("x", "zb"))
-    next_x = shift(mine, 3)
-    last_x = shift(mine, 1)
-    far_x = shift(mine, 2)
+    near_x, far_x, around_x = [swap(mine, "x", 4, k) for k in (1, 2, 3)]
     over_x = over_x.astype(jnp.float32).sum(0).astype(jnp.bfloat16)
     over_z = exchange(over_x.reshape(4, 16, units), "za")
     hidden_grad = over_z.astype(jnp.float32).sum(0)
 
-    all_hidden = jnp.concatenate([mine, next_x, far_x, last_x])
-    rolled = lax.dynamic_slice_in_dim(jnp.concatenate([by_x, by_x]), x, 4).reshape(512, width)
+    all_hidden = jnp.concatenate([mine, far_x, around_x, near_x])
+    rolled = jnp.concatenate([lax.dynamic_slice_in_dim(by_x, x ^ k, 1) for k in (0, 2, 3, 1)]).reshape(512, width)
     weight_grad = lax.dot_general(
         all_hidden, rolled, (((0,), (0,)), ((), ())), preferred_element_type=jnp.float32
     ).astype(jnp.bfloat16)

time: 100 us -> 100 us (level)
    ppermute x3 -> x0, starting transfers between devices: 10.4 us -> none  [shift(): return lax.ppermute(block, 'x', [(i, (i + k) % 4) for i in range(4)])]
    ppermute x2 -> x5, starting transfers between devices: 13.6 us -> 23.4 us  [swap(): return lax.ppermute(block, axis, [(i, i ^ stride) for i in range(size)])]
    ppermute x2 -> x5, waiting for transfers between devices: 7.07 us -> 13.7 us  [swap(): return lax.ppermute(block, axis, [(i, i ^ stride) for i in range(size)])]
    ppermute x3 -> x0, waiting for transfers between devices: 6.01 us -> none  [shift(): return lax.ppermute(block, 'x', [(i, (i + k) % 4) for i in range(4)])]
where the time goes in v6:
time: 100 us; the launch traced here: 99.7 us
  starting transfers between devices  54.7 us (55%)
  waiting for transfers between devices  29.4 us (29%)
  matrix products  7.61 us (8%)
  local copies, waits for them, and re-layouts  4.44 us (4%)
  other arithmetic  2.74 us (3%)
    all_to_all x4, starting transfers between devices, exchange(): return lax.all_to_all(parts, axes, split_axis=0, concat_axis=0)  31.3 us
    ppermute x5, starting transfers between devices, swap(): return lax.ppermute(block, axis, [(i, i ^ stride) for i in range(size)])  23.4 us
    all_to_all x4, waiting for transfers between devices, exchange(): return lax.all_to_all(parts, axes, split_axis=0, concat_axis=0)  15.7 us
    ppermute x5, waiting for transfers between devices, swap(): return lax.ppermute(block, axis, [(i, i ^ stride) for i in range(size)])  13.7 us
    dot_general x1, matrix products, per_device(): lax.dot_general(all_hidden, rolled, (((0,), (0,)), ((), ())), preferred_e...  3.43 us
    unnamed x11, local copies, waits for them, and re-layouts  2.78 us
    dot_general x1, matrix products, per_device(): lax.dot_general(by_part, weight, (((1,), (1,)), ((), ())), preferred_elem...  2.32 us
  transfers between devices with their start and end apart: 9, of which 5 were waited for; matrix products, arithmetic and copies ran while one was open for 9% of the time, Pallas kernels for 0%

profile of v6, /device:TPU:2, one launch (start us, length us, event | category | flops | bytes accessed | tf_op | source)
XLA Modules:
  0.0 99.7 jit_solution(15708773684958182813)
XLA Ops:
  0.6 0.0 copy-start
  0.6 0.9 fusion.8
  1.6 0.7 broadcast_in_dim.4
  2.3 11.2 %all-to-all-start = ((bf16[4,16,1664]{2,1,0:T(8,128)(2,1)}), bf16[4,16,1664]{2,1,0:T(8,128)(2,1)S(1)}, u32[]{:S(2)}, u32[]{:S(2)}) async-start(bf16[4,16,1664]{2,1,0:T(8,128)(2,1)} %broadcast_in_dim.4), calls=%async_computation | async-start | bytes 425984 | tf_op jit(solution)/shard_map/all_to_all | solution.py:10
  13.4 9.1 %collective-permute-start = (bf16[32,512]{1,0:T(8,128)(2,1)}, bf16[32,512]{1,0:T(8,128)(2,1)S(1)}, u32[]{:S(2)}, u32[]{:S(2)}) collective-permute-start(bf16[32,512]{1,0:T(8,128)(2,1)} %param.5), channel_id=1, source_target_pairs={{0,64},{64,0},{1,65},{65,1},{2,66},{66,2},{3,67},{67,3},{4,68},{68... | collective-permute-start | bytes 98312 | tf_op jit(solution)/shard_map/ppermute | solution.py:14
  22.5 2.8 %copy.14 = bf16[1664,512]{0,1:T(8,128)(2,1)S(1)} copy(bf16[1664,512]{1,0:T(8,128)(2,1)} %param.8) | data formatting | bytes 3407872 | tf_op args[3]
  25.3 0.0 copy-start.4
  25.3 1.9 %fusion = bf16[1664,512]{0,1:T(8,128)(2,1)} fusion(bf16[1664,512]{0,1:T(8,128)(2,1)S(1)} %copy.14, f32[16,1664]{1,0:T(8,128)S(1)} %copy-done, s32[512]{0:T(512)S(1)} %add_select_fusion), kind=kOutput, calls=%fused_computation.1 | convolution fusion | flops 29827072 | bytes 3516416 | tf_op jit(solution)/shard_map/dot_general | solution.py:34
  27.2 1.2 %collective-permute-done = bf16[32,512]{1,0:T(8,128)(2,1)S(1)} collective-permute-done((bf16[32,512]{1,0:T(8,128)(2,1)}, bf16[32,512]{1,0:T(8,128)(2,1)S(1)}, u32[]{:S(2)}, u32[]{:S(2)}) %collective-permute-start) | collective-permute-done | bytes 32800 | tf_op jit(solution)/shard_map/ppermute | solution.py:14
  28.4 0.0 copy-start.1
  28.4 0.0 all-to-all-done
  28.4 0.8 broadcast_in_dim.5
  29.2 4.5 %all-to-all-start.1 = ((bf16[8,2,32,512]{3,2,1,0:T(8,128)(2,1)}), bf16[8,2,32,512]{3,2,1,0:T(8,128)(2,1)S(1)}, u32[]{:S(2)}, u32[]{:S(2)}) async-start(bf16[8,2,32,512]{3,2,1,0:T(8,128)(2,1)} %broadcast_in_dim.5), calls=%async_computation.1 | async-start | bytes 1048576 | tf_op jit(solution)/shard_map/all_to_all | solution.py:10
  33.7 4.5 %collective-permute-start.1 = (bf16[4,16,1664]{2,1,0:T(8,128)(2,1)S(1)}, bf16[4,16,1664]{2,1,0:T(8,128)(2,1)S(1)}, u32[]{:S(2)}, u32[]{:S(2)}) collective-permute-start(bf16[4,16,1664]{2,1,0:T(8,128)(2,1)S(1)} %all-to-all-done), channel_id=1, source_target_pairs={{0,4},{4,0},{1,5},{5,1},{2,6},{6,2},{3,7},{7,3},{8,12},{12,8},{9,1... | collective-permute-start | bytes 638984 | tf_op jit(solution)/shard_map/ppermute | solution.py:14
  38.2 5.9 %collective-permute-done.1 = bf16[4,16,1664]{2,1,0:T(8,128)(2,1)S(1)} collective-permute-done((bf16[4,16,1664]{2,1,0:T(8,128)(2,1)S(1)}, bf16[4,16,1664]{2,1,0:T(8,128)(2,1)S(1)}, u32[]{:S(2)}, u32[]{:S(2)}) %collective-permute-start.1) | collective-permute-done | bytes 213024 | tf_op jit(solution)/shard_map/ppermute | solution.py:14
  44.1 0.1 maximum_select_fusion
  44.2 0.0 all-to-all-done.1
  44.2 2.3 %convolution_convert_fusion.1 = bf16[512,1664]{1,0:T(8,128)(2,1)} fusion(bf16[512,512]{1,0:T(8,128)(2,1)S(1)} %bitcast.29, bf16[1664,512]{0,1:T(8,128)(2,1)S(1)} %copy-done.1), kind=kOutput, calls=%fused_computation.3 | convolution fusion | flops 873267200 | bytes 3932160 | tf_op jit(solution)/shard_map/dot_general | solution.py:43
  46.6 6.7 %all-to-all-start.2 = ((bf16[8,64,1664]{2,1,0:T(8,128)(2,1)}), bf16[8,64,1664]{2,1,0:T(8,128)(2,1)S(1)}, u32[]{:S(2)}, u32[]{:S(2)}) async-start(bf16[8,64,1664]{2,1,0:T(8,128)(2,1)} %bitcast.26), calls=%async_computation.2 | async-start | bytes 3407872 | tf_op jit(solution)/shard_map/all_to_all | solution.py:10
  53.3 1.9 %collective-permute-start.4 = (bf16[128,1664]{1,0:T(8,128)(2,1)S(1)}, bf16[128,1664]{1,0:T(8,128)(2,1)S(1)}, u32[]{:S(2)}, u32[]{:S(2)}) collective-permute-start(bf16[128,1664]{1,0:T(8,128)(2,1)S(1)} %bitcast.30), channel_id=1, source_target_pairs={{0,1},{1,0},{2,3},{3,2},{4,5},{5,4},{6,7},{7,6},{8,9},{9,8},{10,11... | collective-permute-start | bytes 1277960 | tf_op jit(solution)/shard_map/ppermute | solution.py:14
  55.2 4.5 %collective-permute-start.3 = (bf16[128,1664]{1,0:T(8,128)(2,1)S(1)}, bf16[128,1664]{1,0:T(8,128)(2,1)}, u32[]{:S(2)}, u32[]{:S(2)}) collective-permute-start(bf16[128,1664]{1,0:T(8,128)(2,1)S(1)} %bitcast.31), channel_id=1, source_target_pairs={{0,3},{1,2},{2,1},{3,0},{4,7},{5,6},{6,5},{7,4},{8,11},{9,10},{10,... | collective-permute-start | bytes 1277960 | tf_op jit(solution)/shard_map/ppermute | solution.py:14
  59.8 3.4 %collective-permute-start.2 = (bf16[128,1664]{1,0:T(8,128)(2,1)S(1)}, bf16[128,1664]{1,0:T(8,128)(2,1)}, u32[]{:S(2)}, u32[]{:S(2)}) collective-permute-start(bf16[128,1664]{1,0:T(8,128)(2,1)S(1)} %bitcast.32), channel_id=1, source_target_pairs={{0,2},{1,3},{2,0},{3,1},{4,6},{5,7},{6,4},{7,5},{8,10},{9,11},{10,... | collective-permute-start | bytes 1277960 | tf_op jit(solution)/shard_map/ppermute | solution.py:14
  63.1 12.3 %all-to-all-done.2 = bf16[8,64,1664]{2,1,0:T(8,128)(2,1)S(1)} async-done(((bf16[8,64,1664]{2,1,0:T(8,128)(2,1)}), bf16[8,64,1664]{2,1,0:T(8,128)(2,1)S(1)}, u32[]{:S(2)}, u32[]{:S(2)}) %all-to-all-start.2) | async-done | bytes 1703968 | tf_op jit(solution)/shard_map/all_to_all | solution.py:10
  75.4 1.0 reduce_sum.21
  76.4 8.9 %all-to-all-start.3 = ((bf16[4,16,1664]{2,1,0:T(8,128)(2,1)}), bf16[4,16,1664]{2,1,0:T(8,128)(2,1)S(1)}, u32[]{:S(2)}, u32[]{:S(2)}) async-start(bf16[4,16,1664]{2,1,0:T(8,128)(2,1)} %bitcast.13), calls=%async_computation.3 | async-start | bytes 425984 | tf_op jit(solution)/shard_map/all_to_all | solution.py:10
  85.4 0.1 pad_maximum_fusion
  85.5 0.0 collective-permute-done.4
  85.5 0.0 collective-permute-done.3
  85.5 6.6 %collective-permute-done.2 = bf16[128,1664]{1,0:T(8,128)(2,1)} collective-permute-done((bf16[128,1664]{1,0:T(8,128)(2,1)S(1)}, bf16[128,1664]{1,0:T(8,128)(2,1)}, u32[]{:S(2)}, u32[]{:S(2)}) %collective-permute-start.2) | collective-permute-done | bytes 426016 | tf_op jit(solution)/shard_map/ppermute | solution.py:14
  92.1 3.4 %convolution_convert_fusion = bf16[1664,512]{1,0:T(8,128)(2,1)} fusion(bf16[512,512]{1,0:T(8,128)(2,1)S(1)} %bitcast.28, bf16[128,1664]{1,0:T(8,128)(2,1)S(1)} %collective-permute-done.4, bf16[128,1664]{1,0:T(8,128)(2,1)} %collective-permute-done.3, bf16[128,1664]{1,0:T(8,128)(2,1)} %collective-permute-done.2, bf16[128,1664]{1,0:T(8,128)(2,1)S(1)} %bitcast.33), kind=kOutput, calls=%fused_computation.2 | convolution fusion | flops 880082944 | bytes 3932160 | tf_op jit(solution)/shard_map/dot_general | solution.py:56
  95.6 3.4 %all-to-all-done.3 = bf16[4,16,1664]{2,1,0:T(8,128)(2,1)S(1)} async-done(((bf16[4,16,1664]{2,1,0:T(8,128)(2,1)}), bf16[4,16,1664]{2,1,0:T(8,128)(2,1)S(1)}, u32[]{:S(2)}, u32[]{:S(2)}) %all-to-all-start.3) | async-done | bytes 213024 | tf_op jit(solution)/shard_map/all_to_all | solution.py:10
  99.0 0.7 multiply_convert_fusion
  (13 shorter events, 0.2 us)
Async XLA Ops:
  0.6 24.7 %copy-start = (f32[16,1664]{1,0:T(8,128)S(1)}, f32[16,1664]{1,0:T(8,128)}, u32[]{:S(2)}) copy-start(f32[16,1664]{1,0:T(8,128)} %param.9) | copy-start | bytes 319492
  2.3 26.1 %all-to-all-start = ((bf16[4,16,1664]{2,1,0:T(8,128)(2,1)}), bf16[4,16,1664]{2,1,0:T(8,128)(2,1)S(1)}, u32[]{:S(2)}, u32[]{:S(2)}) async-start(bf16[4,16,1664]{2,1,0:T(8,128)(2,1)} %broadcast_in_dim.4), calls=%async_computation | async-start | bytes 425984 | tf_op jit(solution)/shard_map/all_to_all | solution.py:10
  13.4 14.9 %collective-permute-start = (bf16[32,512]{1,0:T(8,128)(2,1)}, bf16[32,512]{1,0:T(8,128)(2,1)S(1)}, u32[]{:S(2)}, u32[]{:S(2)}) collective-permute-start(bf16[32,512]{1,0:T(8,128)(2,1)} %param.5), channel_id=1, source_target_pairs={{0,64},{64,0},{1,65},{65,1},{2,66},{66,2},{3,67},{67,3},{4,68},{68... | collective-permute-start | bytes 98312 | tf_op jit(solution)/shard_map/ppermute | solution.py:14
  25.3 3.0 %copy-start.4 = (bf16[32,512]{1,0:T(8,128)(2,1)S(1)}, bf16[32,512]{1,0:T(8,128)(2,1)}, u32[]{:S(2)}) copy-start(bf16[32,512]{1,0:T(8,128)(2,1)} %param.5) | copy-start | bytes 98308
  28.4 15.9 %copy-start.1 = (bf16[1664,512]{0,1:T(8,128)(2,1)S(1)}, bf16[1664,512]{0,1:T(8,128)(2,1)}, u32[]{:S(2)}) copy-start(bf16[1664,512]{0,1:T(8,128)(2,1)} %fusion) | copy-start | bytes 5111812
  29.2 14.9 %all-to-all-start.1 = ((bf16[8,2,32,512]{3,2,1,0:T(8,128)(2,1)}), bf16[8,2,32,512]{3,2,1,0:T(8,128)(2,1)S(1)}, u32[]{:S(2)}, u32[]{:S(2)}) async-start(bf16[8,2,32,512]{3,2,1,0:T(8,128)(2,1)} %broadcast_in_dim.5), calls=%async_computation.1 | async-start | bytes 1048576 | tf_op jit(solution)/shard_map/all_to_all | solution.py:10
  33.7 10.4 %collective-permute-start.1 = (bf16[4,16,1664]{2,1,0:T(8,128)(2,1)S(1)}, bf16[4,16,1664]{2,1,0:T(8,128)(2,1)S(1)}, u32[]{:S(2)}, u32[]{:S(2)}) collective-permute-start(bf16[4,16,1664]{2,1,0:T(8,128)(2,1)S(1)} %all-to-all-done), channel_id=1, source_target_pairs={{0,4},{4,0},{1,5},{5,1},{2,6},{6,2},{3,7},{7,3},{8,12},{12,8},{9,1... | collective-permute-start | bytes 638984 | tf_op jit(solution)/shard_map/ppermute | solution.py:14
  46.6 28.9 %all-to-all-start.2 = ((bf16[8,64,1664]{2,1,0:T(8,128)(2,1)}), bf16[8,64,1664]{2,1,0:T(8,128)(2,1)S(1)}, u32[]{:S(2)}, u32[]{:S(2)}) async-start(bf16[8,64,1664]{2,1,0:T(8,128)(2,1)} %bitcast.26), calls=%async_computation.2 | async-start | bytes 3407872 | tf_op jit(solution)/shard_map/all_to_all | solution.py:10
  53.3 32.2 %collective-permute-start.4 = (bf16[128,1664]{1,0:T(8,128)(2,1)S(1)}, bf16[128,1664]{1,0:T(8,128)(2,1)S(1)}, u32[]{:S(2)}, u32[]{:S(2)}) collective-permute-start(bf16[128,1664]{1,0:T(8,128)(2,1)S(1)} %bitcast.30), channel_id=1, source_target_pairs={{0,1},{1,0},{2,3},{3,2},{4,5},{5,4},{6,7},{7,6},{8,9},{9,8},{10,11... | collective-permute-start | bytes 1277960 | tf_op jit(solution)/shard_map/ppermute | solution.py:14
  55.2 30.3 %collective-permute-start.3 = (bf16[128,1664]{1,0:T(8,128)(2,1)S(1)}, bf16[128,1664]{1,0:T(8,128)(2,1)}, u32[]{:S(2)}, u32[]{:S(2)}) collective-permute-start(bf16[128,1664]{1,0:T(8,128)(2,1)S(1)} %bitcast.31), channel_id=1, source_target_pairs={{0,3},{1,2},{2,1},{3,0},{4,7},{5,6},{6,5},{7,4},{8,11},{9,10},{10,... | collective-permute-start | bytes 1277960 | tf_op jit(solution)/shard_map/ppermute | solution.py:14
  59.8 32.4 %collective-permute-start.2 = (bf16[128,1664]{1,0:T(8,128)(2,1)S(1)}, bf16[128,1664]{1,0:T(8,128)(2,1)}, u32[]{:S(2)}, u32[]{:S(2)}) collective-permute-start(bf16[128,1664]{1,0:T(8,128)(2,1)S(1)} %bitcast.32), channel_id=1, source_target_pairs={{0,2},{1,3},{2,0},{3,1},{4,6},{5,7},{6,4},{7,5},{8,10},{9,11},{10,... | collective-permute-start | bytes 1277960 | tf_op jit(solution)/shard_map/ppermute | solution.py:14
  76.4 22.6 %all-to-all-start.3 = ((bf16[4,16,1664]{2,1,0:T(8,128)(2,1)}), bf16[4,16,1664]{2,1,0:T(8,128)(2,1)S(1)}, u32[]{:S(2)}, u32[]{:S(2)}) async-start(bf16[4,16,1664]{2,1,0:T(8,128)(2,1)} %bitcast.13), calls=%async_computation.3 | async-start | bytes 425984 | tf_op jit(solution)/shard_map/all_to_all | solution.py:10
  92.1 6.9 %copy-start.2 = (bf16[16,1664]{1,0:T(8,128)(2,1)S(1)}, bf16[16,1664]{1,0:T(8,128)(2,1)}, u32[]{:S(2)}) copy-start(bf16[16,1664]{1,0:T(8,128)(2,1)} %param.7) | copy-start | bytes 159748
  92.1 6.9 %copy-start.3 = (bf16[16,1664]{1,0:T(8,128)(2,1)S(1)}, bf16[16,1664]{1,0:T(8,128)(2,1)}, u32[]{:S(2)}) copy-start(bf16[16,1664]{1,0:T(8,128)(2,1)} %param.6) | copy-start | bytes 159748
